TPU v7x, 256 devices: a whole 4x4x8 slice. The times are simulated.
256 devices in a mesh: pp: 8 (over y, z_hi), ep: 32 (over x, z_lo, core).
Axes of the slice: x: 4, y: 4, z: 8 (z_hi: 2, z_lo: 4; z = z_hi * 4 + z_lo), core: 2. Of those that a mesh axis runs over, the one named last changes fastest.
Arguments:
- out_grads: bfloat16 [8, 4096, 3584], P('pp', 'ep'), may hold values from -6 to 6
- expert_ids: int32 [8, 4096, 8], P('pp', 'ep'), may hold values from 0 to 31, all different within a row; in each aligned block of 128 rows (0 to 127, 128 to 255, ..., all dimensions but the last counted through in order) at most 48 rows name the same one
- router_logits: float32 [8, 4096, 32], P('pp', 'ep'), may hold values from -6 to 6
- hidden_acts: bfloat16 [8, 32, 1536, 1024], P('pp', 'ep'), may hold values from -6 to 6
- w_down: bfloat16 [8, 32, 1024, 3584], P('pp', 'ep'), may hold values from -0.1875 to 0.1875
- w_router: bfloat16 [8, 32, 3584], P('pp'), may hold values from -0.59765625 to 0.59765625
Outputs:
- incoming: bfloat16 [8, 4096, 3584], P('pp', 'ep')
Inputs may be any that keep to these rules, and one draw needn't show every extreme that they name: `expert_ids`: each row names 8 different experts; among the 128 tokens of one device for one section no expert is named more than 48 times, a bound that some block reaches.
All inputs are finite; a program needn't handle non-finite values.
Results may differ from a plain program's by a relative error of at most 0.0049.
Values may be sent and summed in bfloat16 or wider, within the bound.
A program may use at most 128 MiB of HBM per device.

v0:
```python
import jax
import jax.numpy as jnp
from jax import lax
from jax.sharding import PartitionSpec as P


def passed_along(x, axis, by):
    size = lax.axis_size(axis)
    pairs = [(i, i + by) for i in range(size) if 0 <= i + by < size]
    return lax.ppermute(x, axis, pairs)


def slot_ranks(chosen, num_experts):
    flat_ids = chosen.reshape(-1)
    onehot = (flat_ids[:, None] == jnp.arange(num_experts, dtype=jnp.int32)[None, :]).astype(
        jnp.int32
    )
    before = jnp.cumsum(onehot, axis=0) - onehot
    return jnp.sum(before * onehot, axis=1).reshape(chosen.shape)


def router_grad(score_grad, chosen, logits, router_weight):
    num_experts = logits.shape[1]
    affinity = jax.nn.sigmoid(logits)
    picked = jnp.take_along_axis(affinity, chosen, axis=1)
    picked_sum = jnp.sum(picked, axis=1, keepdims=True)
    weight = picked / picked_sum
    mean_grad = jnp.sum(weight * score_grad, axis=1, keepdims=True)
    logit_grad = (score_grad - mean_grad) / picked_sum * picked * (1.0 - picked)
    marks = (chosen[:, :, None] == jnp.arange(num_experts, dtype=jnp.int32)[None, None, :]).astype(
        jnp.float32
    )
    logit_table = jnp.sum(marks * logit_grad[:, :, None], axis=1).astype(jnp.bfloat16)
    return jnp.dot(logit_table, router_weight, preferred_element_type=jnp.float32).astype(
        jnp.bfloat16
    )


def on_device(out_grads, expert_ids, router_logits, hidden_acts, w_down, w_router):
    members = lax.axis_size("ep")
    num_experts = w_router.shape[1]
    features = out_grads.shape[2]
    chosen = expert_ids[0]
    places = slot_ranks(chosen, num_experts)
    upstream = out_grads[0]
    activations = hidden_acts[0, 0]
    weight = w_down[0, 0]
    slot_depth = activations.shape[0] // members
    produced = jnp.dot(activations, weight, preferred_element_type=jnp.float32).reshape(
        members, slot_depth, features
    )
    returned = lax.all_to_all(produced, "ep", split_axis=0, concat_axis=0, tiled=True)
    gathered = returned[chosen, places]
    score_grad = jnp.sum(gathered * upstream.astype(jnp.float32)[:, None, :], axis=2)
    result = router_grad(score_grad, chosen, router_logits[0], w_router[0])
    earlier = passed_along(result, "pp", -1)
    return earlier[None]


def solution(mesh):
    in_specs = (
        P("pp", "ep", None),
        P("pp", "ep", None),
        P("pp", "ep", None),
        P("pp", "ep", None, None),
        P("pp", "ep", None, None),
        P("pp", None, None),
    )
    out_specs = P("pp", "ep", None)
    return jax.shard_map(
        on_device, mesh=mesh, in_specs=in_specs, out_specs=out_specs, check_vma=False
    )
```

profile of v0, /device:TPU:8, one launch (start us, length us, event | category | flops | bytes accessed | tf_op | source)
XLA Modules:
  0.0 594.3 jit_solution(16782230487459830390)
XLA Ops:
  0.0 0.0 copy-start
  0.0 1.9 copy-done
  1.9 18.1 %fusion.1 = f32[32,48,3584]{2,1,0:T(8,128)} fusion(bf16[32,48,1024]{2,1,0:T(8,128)(2,1)S(1)} %bitcast.57, bf16[1,1,1024,3584]{3,2,1,0:T(8,128)(2,1)} %param.10), kind=kOutput, calls=%fused_computation.4 | convolution fusion | flops 11274289152 | bytes 32505856 | tf_op jit(solution)/shard_map/dot_general | solution.py:49
  20.0 0.0 copy-start.4
  20.0 0.0 copy-start.5
  20.0 9.0 %all-to-all-start = ((f32[32,48,3584]{2,1,0:T(8,128)}), f32[32,48,3584]{2,1,0:T(8,128)}, u32[]{:S(2)}, u32[]{:S(2)}) async-start(f32[32,48,3584]{2,1,0:T(8,128)} %fusion.1), calls=%async_computation | async-start | bytes 44040192 | tf_op jit(solution)/shard_map/all_to_all | solution.py:52
  29.0 0.0 copy-done.4
  29.0 0.1 copy.29
  29.1 0.1 eq.48
  29.2 0.1 eq.44
  29.3 9.0 %reduce-window.6 = s32[32,8,128]{2,1,0:T(8,128)S(1)} reduce-window(s32[32,8,128]{2,1,0:T(8,128)S(1)} %fusion.7, s32[]{:T(128)} %constant.11.clone.1), window={size=1x1x128 pad=0_0x0_0x127_0}, to_apply=%region_0.0 | reduce-window | flops 4161536 | bytes 262148 | tf_op jit(solution)/shard_map/reduce-window
  38.3 0.1 slice.12
  38.4 0.1 copy.32
  38.6 0.1 copy.33
  38.7 0.1 broadcast_add_fusion
  38.8 0.1 reshape.151
  39.0 0.1 reshape.153
  39.1 0.1 reshape.159
  39.1 0.0 copy-done.5
  39.2 0.0 copy-start.2
  39.2 7.0 %gather_fusion.1 = f32[1024]{0:T(1024)S(1)} fusion(f32[128,32]{0,1:T(8,128)S(1)} %divide_bitcast_fusion, s32[1024]{0:T(1024)S(1)} %reshape.159), kind=kCustom, calls=%fused_computation.1 | custom fusion | bytes 16384 | tf_op jit(solution)/shard_map/jit(take_along_axis)/gather | solution.py:25
  46.2 0.1 reshape.162
  46.4 0.0 copy-done.2
  46.4 1.4 bitcast_convert_fusion
  47.8 458.6 %all-to-all-done = f32[32,48,3584]{2,1,0:T(8,128)} async-done(((f32[32,48,3584]{2,1,0:T(8,128)}), f32[32,48,3584]{2,1,0:T(8,128)}, u32[]{:S(2)}, u32[]{:S(2)}) %all-to-all-start) | async-done | bytes 22020128 | tf_op jit(solution)/shard_map/all_to_all | solution.py:52
  506.4 0.0 copy-start.1
  506.4 32.9 %gather_fusion = f32[1024,3584]{1,0:T(8,128)} fusion(f32[32,48,3584]{2,1,0:T(8,128)} %all-to-all-done, s32[1024]{0:T(1024)S(1)} %reshape.153), kind=kCustom, calls=%fused_computation | custom fusion | bytes 29368320 | tf_op jit(solution)/shard_map/gather | solution.py:53
  539.3 0.0 copy-start.3
  539.3 6.4 %fusion = f32[128,8]{1,0:T(8,128)S(1)} fusion(f32[1024,3584]{1,0:T(8,128)} %gather_fusion, f32[128,3584]{1,0:T(8,128)} %bitcast_convert_fusion), kind=kLoop, calls=%fused_computation.3 | loop fusion | flops 7339008 | bytes 16519168 | tf_op jit(solution)/shard_map/reduce_sum | solution.py:54
  545.9 0.0 copy-done.3
  545.9 0.4 convolution_convert_fusion
  546.3 6.3 %collective-permute-start = (bf16[128,3584]{1,0:T(8,128)(2,1)S(1)}, bf16[128,3584]{1,0:T(8,128)(2,1)S(1)}, u32[]{:S(2)}, u32[]{:S(2)}) collective-permute-start(bf16[128,3584]{1,0:T(8,128)(2,1)S(1)} %convolution_convert_fusion), channel_id=1, source_target_pairs={{32,0},{64,32},{96,64},{128,96},{160,128},{192,160},{224,192},{33,... | collective-permute-start | bytes 2752520 | tf_op jit(solution)/shard_map/ppermute | solution.py:10
  552.6 40.7 %collective-permute-done = bf16[128,3584]{1,0:T(8,128)(2,1)S(1)} collective-permute-done((bf16[128,3584]{1,0:T(8,128)(2,1)S(1)}, bf16[128,3584]{1,0:T(8,128)(2,1)S(1)}, u32[]{:S(2)}, u32[]{:S(2)}) %collective-permute-start) | collective-permute-done | bytes 917536 | tf_op jit(solution)/shard_map/ppermute | solution.py:10
  593.4 0.9 copy.40
  594.3 0.0 copy-done.1
  (12 shorter events, 0.3 us)
Async XLA Ops:
  0.0 1.9 copy-start
  20.0 9.0 %copy-start.4 = (s32[1,128,8]{1,2,0:T(8,128)S(1)}, s32[1,128,8]{1,2,0:T(8,128)}, u32[]{:S(2)}) copy-start(s32[1,128,8]{1,2,0:T(8,128)} %param.7) | copy-start | bytes 12292
  20.0 19.2 %copy-start.5 = (f32[1,128,32]{1,2,0:T(8,128)S(1)}, f32[1,128,32]{1,2,0:T(8,128)}, u32[]{:S(2)}) copy-start(f32[1,128,32]{1,2,0:T(8,128)} %param.8) | copy-start | bytes 49156
  20.0 486.4 %all-to-all-start = ((f32[32,48,3584]{2,1,0:T(8,128)}), f32[32,48,3584]{2,1,0:T(8,128)}, u32[]{:S(2)}, u32[]{:S(2)}) async-start(f32[32,48,3584]{2,1,0:T(8,128)} %fusion.1), calls=%async_computation | async-start | bytes 44040192 | tf_op jit(solution)/shard_map/all_to_all | solution.py:52
  39.2 7.2 %copy-start.2 = (bf16[1,128,3584]{2,1,0:T(8,128)(2,1)S(1)}, bf16[1,128,3584]{2,1,0:T(8,128)(2,1)}, u32[]{:S(2)}) copy-start(bf16[1,128,3584]{2,1,0:T(8,128)(2,1)} %param.6) | copy-start | bytes 2752516
  506.4 87.9 %copy-start.1 = (bf16[1,1,1536,1024]{3,2,1,0:T(8,128)(2,1)S(1)}, bf16[1,1,1536,1024]{3,2,1,0:T(8,128)(2,1)}, u32[]{:S(2)}) copy-start(bf16[1,1,1536,1024]{3,2,1,0:T(8,128)(2,1)} %param.9) | copy-start | bytes 9437188
  539.3 6.6 %copy-start.3 = (bf16[1,32,3584]{2,1,0:T(8,128)(2,1)S(1)}, bf16[1,32,3584]{2,1,0:T(8,128)(2,1)}, u32[]{:S(2)}) copy-start(bf16[1,32,3584]{2,1,0:T(8,128)(2,1)} %param.11) | copy-start | bytes 688132
  546.3 47.1 %collective-permute-start = (bf16[128,3584]{1,0:T(8,128)(2,1)S(1)}, bf16[128,3584]{1,0:T(8,128)(2,1)S(1)}, u32[]{:S(2)}, u32[]{:S(2)}) collective-permute-start(bf16[128,3584]{1,0:T(8,128)(2,1)S(1)} %convolution_convert_fusion), channel_id=1, source_target_pairs={{32,0},{64,32},{96,64},{128,96},{160,128},{192,160},{224,192},{33,... | collective-permute-start | bytes 2752520 | tf_op jit(solution)/shard_map/ppermute | solution.py:10
where the time goes:
time: 595 us; the launch traced here: 594 us
  waiting for transfers between devices  499 us (84%)
  local copies, waits for them, and re-layouts  43.8 us (7%)
  matrix products  18.5 us (3%)
  other arithmetic  17.2 us (3%)
  starting transfers between devices  15.3 us (3%)
    all_to_all x1, waiting for transfers between devices, on_device(): lax.all_to_all(produced, 'ep', split_axis=0, concat_axis=0, tiled=True)  459 us
    ppermute x1, waiting for transfers between devices, passed_along(): return lax.ppermute(x, axis, pairs)  40.7 us
    gather x1, local copies, waits for them, and re-layouts, on_device(): gathered = returned[chosen, places]  32.9 us
    dot_general x1, matrix products, on_device(): jnp.dot(activations, weight, preferred_element_type=jnp.float32)  18.1 us
  transfers between devices with their start and end apart: 2, of which 2 were waited for; matrix products, arithmetic and copies ran while one was open for 3% of the time, Pallas kernels for 0%

commit v1 on v0

v1 whole, which is shorter than its diff:
```python
import jax
import jax.numpy as jnp
from jax import lax
from jax.sharding import PartitionSpec as P


def passed_along(x, axis, by):
    size = lax.axis_size(axis)
    pairs = [(i, i + by) for i in range(size) if 0 <= i + by < size]
    return lax.ppermute(x, axis, pairs)


def rank_table(chosen, num_experts):
    tokens = chosen.shape[0]
    hits = chosen[:, :, None] == jnp.arange(num_experts, dtype=jnp.int32)[None, None, :]
    named = jnp.any(hits, axis=1)
    earlier = jnp.tril(jnp.ones((tokens, tokens), jnp.bfloat16), -1)
    before = jnp.dot(earlier, named.astype(jnp.bfloat16), preferred_element_type=jnp.float32)
    return named, jnp.where(named, before, -1.0)


def on_device(out_grads, expert_ids, router_logits, hidden_acts, w_down, w_router):
    members = lax.axis_size("ep")
    num_experts = w_router.shape[1]
    chosen = expert_ids[0]
    named, ranks = rank_table(chosen, num_experts)
    upstream = lax.all_gather(out_grads[0], "ep", axis=0)
    rank_rows = lax.all_to_all(ranks.T, "ep", split_axis=0, concat_axis=0, tiled=True)
    next_router = passed_along(w_router[0], "pp", -1)
    activations = hidden_acts[0, 0]
    depth = activations.shape[0] // members
    produced = jnp.dot(
        activations, w_down[0, 0], preferred_element_type=jnp.float32
    ).astype(jnp.bfloat16)
    produced = produced.reshape(members, depth, -1)
    cross = lax.dot_general(
        upstream,
        produced,
        (((2,), (2,)), ((0,), (0,))),
        preferred_element_type=jnp.float32,
    )
    mask = rank_rows[:, :, None] == jnp.arange(depth, dtype=jnp.float32)[None, None, :]
    scores = jnp.sum(jnp.where(mask, cross, 0.0), axis=2)
    score_grad = lax.all_to_all(scores, "ep", split_axis=0, concat_axis=0, tiled=True).T
    picked = jnp.where(named, jax.nn.sigmoid(router_logits[0]), 0.0)
    picked_sum = jnp.sum(picked, axis=1, keepdims=True)
    mean_grad = jnp.sum(picked / picked_sum * score_grad, axis=1, keepdims=True)
    table = (score_grad - mean_grad) / picked_sum * picked * (1.0 - picked)
    table = passed_along(table.astype(jnp.bfloat16), "pp", -1)
    result = jnp.dot(table, next_router, preferred_element_type=jnp.float32)
    return result.astype(jnp.bfloat16)[None]


def solution(mesh):
    in_specs = (
        P("pp", "ep", None),
        P("pp", "ep", None),
        P("pp", "ep", None),
        P("pp", "ep", None, None),
        P("pp", "ep", None, None),
        P("pp", None, None),
    )
    out_specs = P("pp", "ep", None)
    return jax.shard_map(
        on_device, mesh=mesh, in_specs=in_specs, out_specs=out_specs, check_vma=False
    )
```

time: 595 us -> 235 us (0.39)
  waiting for transfers between devices: 499 us -> 158 us
  local copies, waits for them, and re-layouts: 43.8 us -> 0.01 us
  matrix products: 18.5 us -> 36.8 us
  other arithmetic: 17.2 us -> 1.01 us
  between operations: 0.18 us -> 13.5 us
  starting transfers between devices: 15.3 us -> 25.5 us
    all_to_all x1 -> x2, waiting for transfers between devices: 459 us -> 7.6 us  [the longest x1 7.6 us: on_device(): lax.all_to_all(scores, 'ep', split_axis=0, concat_axis=0, tiled=True)]
    all_gather x0 -> x1, waiting for transfers between devices: none -> 144 us  [on_device(): upstream = lax.all_gather(out_grads[0], 'ep', axis=0)]
    gather x5 -> x0, local copies, waits for them, and re-layouts: 40.1 us -> none  [the longest x1 32.9 us: on_device(): gathered = returned[chosen, places]]
    ppermute x1 -> x2, waiting for transfers between devices: 40.7 us -> 5.21 us  [passed_along(): return lax.ppermute(x, axis, pairs)]
    dot_general x2 -> x4, matrix products: 18.5 us -> 36.8 us  [the longest x1 17.7 us: on_device(): lax.dot_general(upstream, produced, (((2,), (2,)), ((0,), (0,))), preferr...]
    another operation x3 -> x0, other arithmetic: 9.15 us -> none
    reduce_sum x5 -> x2, other arithmetic: 6.57 us -> 0.06 us  [the longest x1 0.03 us: on_device(): mean_grad = jnp.sum(picked / picked_sum * score_grad, axis=1, keepdims=True)]
    all_to_all x1 -> x2, starting transfers between devices: 9 us -> 15 us  [the longest x1 8.75 us: on_device(): lax.all_to_all(ranks.T, 'ep', split_axis=0, concat_axis=0, tiled=True)]
  transfers between devices with their start and end apart: 2 -> 5, of which waited for: 2 -> 3; matrix products, arithmetic and copies ran while one was open for 3% -> 16% of each run, Pallas kernels for 0% -> 0%
where the time goes in v1:
time: 235 us; the launch traced here: 234 us
  waiting for transfers between devices  158 us (67%)
  matrix products  36.8 us (16%)
  starting transfers between devices  25.5 us (11%)
  between operations  13.5 us (6%)
    all_gather x1, waiting for transfers between devices, on_device(): upstream = lax.all_gather(out_grads[0], 'ep', axis=0)  144 us
    dot_general x1, matrix products, on_device(): lax.dot_general(upstream, produced, (((2,), (2,)), ((0,), (0,))), preferr...  17.7 us
    dot_general x1, matrix products, on_device(): jnp.dot(activations, w_down[0, 0], preferred_element_type=jnp.float32)  16.9 us
    ppermute x2, starting transfers between devices, passed_along(): return lax.ppermute(x, axis, pairs)  10.5 us
    all_to_all x1, starting transfers between devices, on_device(): lax.all_to_all(ranks.T, 'ep', split_axis=0, concat_axis=0, tiled=True)  8.75 us
    all_to_all x1, waiting for transfers between devices, on_device(): lax.all_to_all(scores, 'ep', split_axis=0, concat_axis=0, tiled=True)  7.6 us
    all_to_all x1, starting transfers between devices, on_device(): lax.all_to_all(scores, 'ep', split_axis=0, concat_axis=0, tiled=True)  6.24 us
    ppermute x2, waiting for transfers between devices, passed_along(): return lax.ppermute(x, axis, pairs)  5.21 us
  transfers between devices with their start and end apart: 5, of which 3 were waited for; matrix products, arithmetic and copies ran while one was open for 16% of the time, Pallas kernels for 0%

profile of v1, /device:TPU:8, one launch (start us, length us, event | category | flops | bytes accessed | tf_op | source)
XLA Modules:
  0.0 234.3 jit_solution(10863268338311607222)
XLA Ops:
  6.5 0.0 copy-start
  6.5 0.0 all-gather.2.cloned.1.call-start
  6.5 0.7 all-gather.2.cloned.1.call-update
  7.3 0.9 fusion.5
  8.2 0.8 convolution_select_fusion
  9.0 8.8 %all-to-all-start = ((f32[32,1,128]{2,1,0:T(1,128)}), f32[32,1,128]{2,1,0:T(1,128)S(1)}, u32[]{:S(2)}, u32[]{:S(2)}) async-start(f32[32,1,128]{2,1,0:T(1,128)} %bitcast.3), calls=%async_computation | async-start | bytes 32768 | tf_op jit(solution)/shard_map/all_to_all | solution.py:28
  17.8 6.3 %collective-permute-start.1 = (bf16[32,3584]{1,0:T(8,128)(2,1)}, bf16[32,3584]{1,0:T(8,128)(2,1)S(1)}, u32[]{:S(2)}, u32[]{:S(2)}) collective-permute-start(bf16[32,3584]{1,0:T(8,128)(2,1)} %bitcast.45), channel_id=1, source_target_pairs={{32,0},{64,32},{96,64},{128,96},{160,128},{192,160},{224,192},{33,... | collective-permute-start | bytes 688136 | tf_op jit(solution)/shard_map/ppermute | solution.py:10
  24.1 0.0 copy-done
  24.1 16.9 %convolution_convert_fusion = bf16[1536,3584]{1,0:T(8,128)(2,1)} fusion(bf16[1,1,1024,3584]{3,2,1,0:T(8,128)(2,1)} %param.10, bf16[1,1,1536,1024]{3,2,1,0:T(8,128)(2,1)S(1)} %copy-done), kind=kOutput, calls=%fused_computation | convolution fusion | flops 11279794176 | bytes 21495808 | tf_op jit(solution)/shard_map/dot_general | solution.py:32
  41.0 0.0 all-to-all-done
  41.0 144.0 %all-gather.2.cloned.1.call-done = bf16[32,128,3584]{2,1,0:T(8,128)(2,1)} async-done(((bf16[1,128,3584]{2,1,0:T(8,128)(2,1)}), bf16[32,128,3584]{2,1,0:T(8,128)(2,1)}) %all-gather.2.cloned.1.call-update) | async-done | bytes 29360144 | tf_op jit(solution)/shard_map/all_gather | solution.py:27
  185.0 0.0 copy-start.1
  185.0 17.7 %fusion.4 = f32[32,128]{1,0:T(8,128)} fusion(bf16[32,48,3584]{2,1,0:T(8,128)(2,1)} %bitcast.40, bf16[32,128,3584]{2,1,0:T(8,128)(2,1)} %all-gather.2.cloned.1.call-done, f32[32,128]{1,0:T(8,128)S(1)} %bitcast.43), kind=kOutput, calls=%fused_computation.7 | convolution fusion | flops 1409871872 | bytes 40402944 | tf_op jit(solution)/shard_map/dot_general | solution.py:36
  202.7 6.2 %all-to-all-start.1 = ((f32[32,1,128]{2,1,0:T(1,128)}), f32[32,1,128]{2,1,0:T(1,128)S(1)}, u32[]{:S(2)}, u32[]{:S(2)}) async-start(f32[32,1,128]{2,1,0:T(1,128)} %bitcast.9), calls=%async_computation.1 | async-start | bytes 32768 | tf_op jit(solution)/shard_map/all_to_all | solution.py:44
  209.0 0.0 copy-done.1
  209.0 7.6 %all-to-all-done.1 = f32[32,1,128]{2,1,0:T(1,128)S(1)} async-done(((f32[32,1,128]{2,1,0:T(1,128)}), f32[32,1,128]{2,1,0:T(1,128)S(1)}, u32[]{:S(2)}, u32[]{:S(2)}) %all-to-all-start.1) | async-done | bytes 16416 | tf_op jit(solution)/shard_map/all_to_all | solution.py:44
  216.7 4.2 %collective-permute-start = (bf16[128,32]{0,1:T(8,128)(2,1)S(1)}, bf16[128,32]{0,1:T(8,128)(2,1)S(1)}, u32[]{:S(2)}, u32[]{:S(2)}) collective-permute-start(bf16[128,32]{0,1:T(8,128)(2,1)S(1)} %multiply_convert_fusion), channel_id=1, source_target_pairs={{32,0},{64,32},{96,64},{128,96},{160,128},{192,160},{224,192},{33,... | collective-permute-start | bytes 24584 | tf_op jit(solution)/shard_map/ppermute | solution.py:10
  220.9 0.0 collective-permute-done.1
  220.9 5.2 %collective-permute-done = bf16[128,32]{0,1:T(8,128)(2,1)S(1)} collective-permute-done((bf16[128,32]{0,1:T(8,128)(2,1)S(1)}, bf16[128,32]{0,1:T(8,128)(2,1)S(1)}, u32[]{:S(2)}, u32[]{:S(2)}) %collective-permute-start) | collective-permute-done | bytes 8224 | tf_op jit(solution)/shard_map/ppermute | solution.py:10
  226.1 1.4 fusion.1
  (4 shorter events, 0.1 us)
Async XLA Ops:
  6.5 17.5 %copy-start = (bf16[1,1,1536,1024]{3,2,1,0:T(8,128)(2,1)S(1)}, bf16[1,1,1536,1024]{3,2,1,0:T(8,128)(2,1)}, u32[]{:S(2)}) copy-start(bf16[1,1,1536,1024]{3,2,1,0:T(8,128)(2,1)} %param.9) | copy-start | bytes 9437188
  6.5 178.5 %all-gather.2.cloned.1.call-start = ((), (), s32[]{:S(2)}) async-start(), calls=%async_computation.2 | async-start | bytes 30277632 | tf_op jit(solution)/shard_map/all_gather | solution.py:27
  9.0 32.0 %all-to-all-start = ((f32[32,1,128]{2,1,0:T(1,128)}), f32[32,1,128]{2,1,0:T(1,128)S(1)}, u32[]{:S(2)}, u32[]{:S(2)}) async-start(f32[32,1,128]{2,1,0:T(1,128)} %bitcast.3), calls=%async_computation | async-start | bytes 32768 | tf_op jit(solution)/shard_map/all_to_all | solution.py:28
  17.8 203.1 %collective-permute-start.1 = (bf16[32,3584]{1,0:T(8,128)(2,1)}, bf16[32,3584]{1,0:T(8,128)(2,1)S(1)}, u32[]{:S(2)}, u32[]{:S(2)}) collective-permute-start(bf16[32,3584]{1,0:T(8,128)(2,1)} %bitcast.45), channel_id=1, source_target_pairs={{32,0},{64,32},{96,64},{128,96},{160,128},{192,160},{224,192},{33,... | collective-permute-start | bytes 688136 | tf_op jit(solution)/shard_map/ppermute | solution.py:10
  185.0 23.9 %copy-start.1 = (f32[1,128,32]{1,2,0:T(8,128)S(1)}, f32[1,128,32]{1,2,0:T(8,128)}, u32[]{:S(2)}) copy-start(f32[1,128,32]{1,2,0:T(8,128)} %param.8) | copy-start | bytes 49156
  202.7 13.9 %all-to-all-start.1 = ((f32[32,1,128]{2,1,0:T(1,128)}), f32[32,1,128]{2,1,0:T(1,128)S(1)}, u32[]{:S(2)}, u32[]{:S(2)}) async-start(f32[32,1,128]{2,1,0:T(1,128)} %bitcast.9), calls=%async_computation.1 | async-start | bytes 32768 | tf_op jit(solution)/shard_map/all_to_all | solution.py:44
  216.7 9.5 %collective-permute-start = (bf16[128,32]{0,1:T(8,128)(2,1)S(1)}, bf16[128,32]{0,1:T(8,128)(2,1)S(1)}, u32[]{:S(2)}, u32[]{:S(2)}) collective-permute-start(bf16[128,32]{0,1:T(8,128)(2,1)S(1)} %multiply_convert_fusion), channel_id=1, source_target_pairs={{32,0},{64,32},{96,64},{128,96},{160,128},{192,160},{224,192},{33,... | collective-permute-start | bytes 24584 | tf_op jit(solution)/shard_map/ppermute | solution.py:10
Sparse Core Ops, SparseCore 0:
  9.2 175.7 all-gather.1

commit v2 on v1

v2 whole, which is shorter than its diff:
```python
import functools

import jax
import jax.numpy as jnp
from jax import lax
from jax.experimental import pallas as pl
from jax.experimental.pallas import tpu as pltpu
from jax.sharding import PartitionSpec as P

MESH = pl.DeviceIdType.MESH
F32, BF16 = jnp.float32, jnp.bfloat16

X, Z, CORES = 4, 4, 2
CHIPS = X * Z
TOK, D, FFW, MOST, EXPERTS = 128, 3584, 1024, 48, 32
WIDE, SLIM = 1408, 384
OFFSET = (0, WIDE, 2 * WIDE + SLIM, 2 * WIDE)
BULK = 2 * WIDE + SLIM
QUARTER = D // X
HALF = D // 2
RANK_ROWS = 16

ORDER = (
    (
        16, 48, 4, 17, 49, 5, 18, 50, 6, 19, 51, 7, 32, 20, 8, 21, 52, 9, 10, 22,
        54, 33, 53, 11, 34, 35, 23, 55, 24, 56, 12, 36, 25, 13, 14, 26, 37, 57, 58, 15,
        27, 59, 40, 28, 30, 62, 31, 41, 60, 63, 46, 47, 38, 29, 61, 39, 42, 43, 44, 45,
    ),
    (
        20, 52, 0, 8, 21, 53, 1, 9, 22, 54, 2, 10, 23, 55, 3, 11, 18, 50, 19, 36,
        16, 12, 51, 48, 24, 13, 14, 26, 58, 17, 56, 15, 27, 59, 34, 30, 35, 49, 25, 62,
        31, 63, 46, 37, 57, 47, 38, 39, 42, 43, 28, 60, 32, 29, 33, 61, 40, 41, 44, 45,
    ),
    (
        24, 56, 12, 4, 25, 57, 13, 5, 26, 58, 14, 6, 27, 59, 15, 7, 30, 62, 31, 40,
        20, 0, 63, 28, 52, 1, 2, 22, 54, 60, 21, 3, 23, 55, 46, 18, 47, 29, 53, 50,
        19, 51, 34, 41, 61, 35, 42, 43, 38, 39, 16, 48, 36, 17, 37, 49, 44, 45, 32, 33,
    ),
    (
        28, 60, 8, 29, 61, 9, 30, 62, 10, 31, 63, 11, 44, 24, 4, 25, 56, 5, 6, 26,
        58, 45, 57, 7, 46, 47, 27, 59, 20, 52, 0, 40, 21, 1, 2, 22, 41, 53, 54, 3,
        23, 55, 36, 16, 18, 50, 19, 37, 48, 51, 34, 35, 42, 17, 49, 43, 38, 39, 32, 33,
    ),
)
EARLY = 8


def programme(z):
    own = [4 * z + p for p in range(4)]
    late = own + list(ORDER[z][:EARLY])
    steps = []
    for code in ORDER[z][EARLY:]:
        if late:
            steps.append(late.pop(0))
        steps.append(code + 64)
    seen = {}
    out = []
    for code in steps:
        shard = code % 64 // 4
        seen[shard] = seen.get(shard, 0) + 1
        out.append(code + (128 if seen[shard] == 4 else 0))
    return tuple(out)


STEPS = tuple(programme(z) for z in range(Z))
COUNT = len(STEPS[0])


def packed(codes):
    words = []
    for k in range(0, len(codes), 3):
        words.append(sum(code << (8 * j) for j, code in enumerate(codes[k : k + 3])))
    return words


def by_row(z, values):
    picked = jnp.int32(values[Z - 1])
    for row in range(Z - 1):
        picked = jnp.where(z == row, jnp.int32(values[row]), picked)
    return picked


def entry(words, i):
    place = lax.div(i, 3)
    while len(words) > 1:
        odd = lax.rem(place, 2) == 1
        halved = []
        for k in range(0, len(words), 2):
            more = k + 1 < len(words)
            halved.append(jnp.where(odd, words[k + 1], words[k]) if more else words[k])
        words, place = halved, lax.div(place, 2)
    turn = lax.rem(i, 3)
    scale = jnp.where(turn == 0, 1, jnp.where(turn == 1, 1 << 8, 1 << 16))
    return lax.rem(lax.div(words[0], scale), 256)


def goes(way, x, z, xo, zo, piece):
    dx = lax.rem(xo - x + X, X)
    odd = lax.rem(piece, 2)
    slim = piece >= 2
    in_line = jnp.logical_or(slim, dx == 0)
    in_row = jnp.logical_or(jnp.logical_not(slim), zo == z)
    if way == 0:
        return in_line & (zo <= z) & (z < Z - 1)
    if way == 1:
        return in_line & (zo >= z) & (z > 0)
    if way == 2:
        return in_row & ((dx == 0) | ((dx == X - 1) & (odd == 0)))
    return in_row & ((dx == 0) | ((dx == 1) & (odd == 1)))


def kernel(
    g_hbm, ids_hbm, logits_hbm, h_hbm, w_hbm, r_hbm,
    st_out, rn_out, pk_out,
    bulk, slim, prod, cross, hbuf, wbuf, acc, sent_scores,
    ids_v, logits_v, picked_v, st, rn, pk,
    load_sem, send_sem, recv_sem, cross_send, cross_recv,
    score_send, score_recv, r_send, r_recv, pk_send, pk_recv,
):
    sections = lax.axis_size("pp")
    s = lax.axis_index("pp")
    me = lax.axis_index("ep")
    core = lax.rem(me, CORES)
    chip = lax.div(me, CORES)
    x, z = lax.div(chip, Z), lax.rem(chip, Z)

    def at(xx, zz, cc=core):
        return (xx * Z + zz) * CORES + cc

    right, left = lax.rem(x + 1, X), lax.rem(x + X - 1, X)
    across = lax.rem(x + 2, X)
    sibling = (s, at(x, z, 1 - core))
    target = (
        (s, at(x, jnp.minimum(z + 1, Z - 1))),
        (s, at(x, jnp.maximum(z - 1, 0))),
        (s, at(right, z)),
        (s, at(left, z)),
    )
    opposite = (s, at(across, z))
    below = jnp.maximum(s - 1, 0)
    above = jnp.minimum(s + 1, sections - 1)

    def load(k, src, dst):
        return pltpu.make_async_copy(src, dst, load_sem.at[k])

    loads = [
        load(0, g_hbm.at[:, pl.ds(0, BULK)], bulk.at[chip]),
        load(1, g_hbm.at[:, pl.ds(BULK, SLIM)], slim.at[chip, pl.ds(0, TOK)]),
        load(2, ids_hbm, ids_v),
        load(3, logits_hbm, logits_v),
        load(4, h_hbm.at[:, 1 - core], hbuf.at[0]),
        load(5, w_hbm.at[:, pl.ds(0, HALF)], wbuf.at[:, pl.ds(0, HALF)]),
        load(6, w_hbm.at[:, pl.ds(HALF, HALF)], wbuf.at[:, pl.ds(HALF, HALF)]),
        load(7, h_hbm.at[:, core], hbuf.at[1]),
    ]
    for copy in loads:
        copy.start()

    barrier = pltpu.get_barrier_semaphore()

    def greet(device):
        pl.semaphore_signal(barrier, inc=1, device_id=device, device_id_type=MESH)

    for device in (target[2], target[3], opposite, sibling):
        greet(device)

    @pl.when(z < Z - 1)
    def _():
        greet(target[0])

    @pl.when(z > 0)
    def _():
        greet(target[1])

    @pl.when(s > 0)
    def _():
        @pl.loop(0, CHIPS)
        def _(q):
            greet((below, q * CORES + core))

    @pl.when(s < sections - 1)
    def _():
        @pl.loop(0, CHIPS)
        def _(q):
            greet((above, q * CORES + core))

    calls = 4 + (z < Z - 1).astype(jnp.int32) + (z > 0).astype(jnp.int32)
    calls = calls + CHIPS * ((s > 0).astype(jnp.int32) + (s < sections - 1).astype(jnp.int32))
    pl.semaphore_wait(barrier, calls)

    def remote(src, dst, send, recv, device):
        return pltpu.make_async_remote_copy(
            src_ref=src, dst_ref=dst, send_sem=send, recv_sem=recv,
            device_id=device, device_id_type=MESH,
        )

    def wide_piece(q, piece):
        return bulk.at[q, :, pl.ds(pl.multiple_of(piece * WIDE, 128), WIDE)]

    def piece_ref(q, kind, piece):
        if kind == 0:
            return wide_piece(q, piece)
        if kind == 1:
            return slim.at[q]
        return bulk.at[q, :, pl.ds(2 * WIDE, SLIM)]

    def passing(way, q, kind, piece):
        ref = piece_ref(q, kind, piece)
        return remote(ref, ref, send_sem.at[way, q, piece], recv_sem.at[q, piece], target[way])

    def pass_on(q, kind, piece):
        xo, zo = lax.div(q, Z), lax.rem(q, Z)
        for way in range(4):

            @pl.when(goes(way, x, z, xo, zo, piece))
            def _(way=way):
                passing(way, q, kind, piece).start()

    rows = pl.ds(pl.multiple_of(core * RANK_ROWS, RANK_ROWS), RANK_ROWS)

    def quarter(xx):
        return pl.ds(pl.multiple_of(xx * QUARTER, 128), QUARTER)

    router_down = remote(
        r_hbm.at[rows, quarter(x)], rn.at[rows, quarter(x)], r_send.at[0], r_recv.at[0], (below, me)
    )

    @pl.when(s > 0)
    def _():
        router_down.start()

    loads[0].wait()
    pass_on(chip, 0, 0)
    pass_on(chip, 0, 1)

    for k in (1, 2, 3):
        loads[k].wait()
    lanes = lax.broadcasted_iota(jnp.int32, (TOK, 128), 1)
    ids = ids_v[...]
    marks = jnp.zeros((TOK, 128), F32)
    for k in range(ids.shape[1]):
        marks = marks + (ids[:, k : k + 1] == lanes).astype(F32)
    named = marks.T[:EXPERTS]
    upper = (
        lax.broadcasted_iota(jnp.int32, (TOK, TOK), 0)
        < lax.broadcasted_iota(jnp.int32, (TOK, TOK), 1)
    ).astype(BF16)
    before = jnp.dot(named.astype(BF16), upper, preferred_element_type=F32)
    ranks = jnp.where(named > 0, before, -1.0).astype(BF16)
    slim[chip, TOK : TOK + RANK_ROWS, :] = jnp.concatenate(
        [ranks[:RANK_ROWS], ranks[RANK_ROWS:], jnp.zeros((RANK_ROWS, SLIM - 2 * TOK), BF16)], axis=1
    )
    pass_on(chip, 1, 2)
    pass_on(chip, 2, 3)
    logits = jnp.concatenate([logits_v[...], jnp.zeros((TOK, 128 - EXPERTS), F32)], axis=1)
    affinity = 1.0 / (1.0 + jnp.exp(-logits.T[:EXPERTS]))
    picked_v[...] = jnp.where(named > 0, affinity, 0.0)
    picked_down = remote(picked_v, pk, pk_send, pk_recv, (below, me))

    @pl.when(s > 0)
    def _():
        picked_down.start()

    steps = [by_row(z, words) for words in zip(*map(packed, STEPS))]
    early = [by_row(z, words) for words in zip(*(packed(row[:EARLY]) for row in ORDER))]

    def outputs(which, half, store):
        lhs = hbuf[which].reshape(CHIPS * MOST, FFW)

        @pl.loop(0, HALF // 256)
        def _(t):
            cols = pl.ds(pl.multiple_of(half * HALF + t * 256, 256), 256)
            out = jnp.dot(lhs, wbuf[:, cols], preferred_element_type=F32)
            store(cols, out.astype(BF16).reshape(CHIPS, MOST, 256))

    def store_cross(cols, value):
        cross[:, :, cols] = value

    def store_own(cols, value):
        prod[:, core, :, cols] = value

    def crossing(half):
        cols = pl.ds(half * HALF, HALF)
        return remote(
            cross.at[:, :, cols], prod.at[:, core, :, cols],
            cross_send.at[half], cross_recv.at[half], sibling,
        )

    loads[4].wait()
    for half in range(2):
        loads[5 + half].wait()
        outputs(0, half, store_cross)
        crossing(half).start()
    loads[7].wait()
    for half in range(2):
        outputs(1, half, store_own)

    def take(q, kind, piece):
        passing(2, q, kind, piece).wait_recv()
        pass_on(q, kind, piece)

    def decode(code):
        shard = lax.rem(code, 64)
        xo = lax.rem(x + lax.div(shard, 16), X)
        zo = lax.rem(lax.div(shard, 4), Z)
        return xo * Z + zo, lax.rem(shard, 4)

    def by_kind(piece, act):
        for kind, cond in ((0, piece < 2), (1, piece == 2), (2, piece == 3)):

            @pl.when(cond)
            def _(kind=kind):
                act(kind, piece if kind == 0 else jnp.int32(kind + 1))

    @pl.loop(0, EARLY)
    def _(i):
        q, piece = decode(entry(early, i))
        by_kind(piece, functools.partial(take, q))

    def spread(k, device):
        ref = rn.at[rows, quarter(x)]
        return remote(ref, ref, r_send.at[1 + k], r_recv.at[1 + k], device)

    def came(k, xx):
        ref = rn.at[rows, quarter(xx)]
        return remote(ref, ref, r_send.at[1 + k], r_recv.at[1 + k], target[2])

    spreads = [spread(0, target[2]), spread(1, target[3]), spread(2, opposite)]
    own_rows = remote(rn.at[rows], rn.at[rows], r_send.at[4], r_recv.at[4], sibling)
    other = pl.ds(pl.multiple_of((1 - core) * RANK_ROWS, RANK_ROWS), RANK_ROWS)
    other_rows = remote(rn.at[other], rn.at[other], r_send.at[4], r_recv.at[4], sibling)

    @pl.when(s < sections - 1)
    def _():
        router_down.wait_recv()
        for copy in spreads:
            copy.start()

    for half in range(2):
        crossing(half).wait_recv()
    acc[...] = jnp.zeros_like(acc)

    def score_copy(q):
        return remote(
            sent_scores.at[q], st.at[chip], score_send.at[q], score_recv.at[chip],
            (below, q * CORES + core),
        )

    first = lax.rem(chip * CORES, RANK_ROWS)
    group = lax.div(chip * CORES, RANK_ROWS)

    def score(q, kind, piece):
        if kind == 0:
            cols = pl.ds(pl.multiple_of(piece * WIDE, 128), WIDE)
            block = bulk[q, :, cols]
        elif kind == 1:
            cols = pl.ds(BULK, SLIM)
            block = slim[q, :TOK, :]
        else:
            cols = pl.ds(2 * WIDE, SLIM)
            block = bulk[q, :, cols]
        lhs = prod[q, :, :, cols].reshape(CORES * MOST, block.shape[1])
        acc[q] += lax.dot_general(
            lhs, block, (((1,), (1,)), ((), ())), preferred_element_type=F32
        )

    def finish(q):
        lane0 = pl.ds(pl.multiple_of(group * TOK, TOK), TOK)
        held = slim[q, pl.ds(TOK, RANK_ROWS), lane0].astype(F32)
        line = lax.broadcasted_iota(jnp.int32, (RANK_ROWS, TOK), 0)
        slot = lax.broadcasted_iota(jnp.int32, (MOST, TOK), 0).astype(F32)
        total = acc[q]
        tile = lax.broadcasted_iota(jnp.int32, (8, TOK), 0)
        result = jnp.zeros((8, TOK), F32)
        for e in range(CORES):
            rank = jnp.sum(jnp.where(line == first + e, held, 0.0), axis=0, keepdims=True)
            part = total[e * MOST : (e + 1) * MOST]
            row = jnp.sum(jnp.where(slot == rank, part, 0.0), axis=0, keepdims=True)
            result = jnp.where(tile == e, row, result)
        sent_scores[q] = result

        @pl.when(s > 0)
        def _():
            score_copy(q).start()

    @pl.loop(0, COUNT)
    def _(i):
        code = entry(steps, i)
        q, piece = decode(code)
        new = lax.rem(lax.div(code, 64), 2) == 1

        def step(kind, which):
            @pl.when(new)
            def _():
                take(q, kind, which)

            score(q, kind, which)

        by_kind(piece, step)

        @pl.when(code >= 128)
        def _():
            finish(q)

        @pl.when((i == COUNT // 2) & (s < sections - 1))
        def _():
            came(0, left).wait_recv()
            came(1, right).wait_recv()
            came(2, across).wait_recv()
            own_rows.start()

    @pl.when(s < sections - 1)
    def _():
        other_rows.wait_recv()
        rn_out[...] = rn[...]
        picked_down.wait_recv()
        pk_out[...] = pk[...]

        @pl.loop(0, CHIPS)
        def _(q):
            remote(
                sent_scores.at[q], st.at[q], score_send.at[q], score_recv.at[q], (below, me)
            ).wait_recv()

        st_out[...] = st[...]

    @pl.when(s == sections - 1)
    def _():
        rn_out[...] = jnp.zeros_like(rn_out)
        pk_out[...] = jnp.zeros_like(pk_out)
        st_out[...] = jnp.zeros_like(st_out)

    for half in range(2):
        crossing(half).wait_send()

    @pl.when(s < sections - 1)
    def _():
        for copy in spreads:
            copy.wait_send()
        own_rows.wait_send()

    @pl.when(s > 0)
    def _():
        router_down.wait_send()
        picked_down.wait_send()

        @pl.loop(0, CHIPS)
        def _(q):
            score_copy(q).wait_send()

    @pl.loop(0, CHIPS)
    def _(q):
        xo, zo = lax.div(q, Z), lax.rem(q, Z)
        for kind, pieces in ((0, (0, 1)), (1, (2,)), (2, (3,))):
            for piece in pieces:
                for way in range(4):

                    @pl.when(goes(way, x, z, xo, zo, piece))
                    def _(kind=kind, piece=piece, way=way):
                        passing(way, q, kind, piece).wait_send()


def exchange(g, ids, logits, h, w, r):
    vmem = pl.BlockSpec(memory_space=pltpu.VMEM)
    dma = pltpu.SemaphoreType.DMA
    return pl.pallas_call(
        kernel,
        out_shape=(
            jax.ShapeDtypeStruct((CHIPS, 8, TOK), F32),
            jax.ShapeDtypeStruct((EXPERTS, D), BF16),
            jax.ShapeDtypeStruct((EXPERTS, TOK), F32),
        ),
        in_specs=[pl.BlockSpec(memory_space=pl.ANY)] * 6,
        out_specs=(vmem,) * 3,
        scratch_shapes=[
            pltpu.VMEM((CHIPS, TOK, BULK), BF16),
            pltpu.VMEM((CHIPS, TOK + RANK_ROWS, SLIM), BF16),
            pltpu.VMEM((CHIPS, CORES, MOST, D), BF16),
            pltpu.VMEM((CHIPS, MOST, D), BF16),
            pltpu.VMEM((CORES, CHIPS, MOST, FFW), BF16),
            pltpu.VMEM((FFW, D), BF16),
            pltpu.VMEM((CHIPS, CORES * MOST, TOK), F32),
            pltpu.VMEM((CHIPS, 8, TOK), F32),
            pltpu.VMEM(ids.shape, jnp.int32),
            pltpu.VMEM(logits.shape, F32),
            pltpu.VMEM((EXPERTS, TOK), F32),
            pltpu.VMEM((CHIPS, 8, TOK), F32),
            pltpu.VMEM((EXPERTS, D), BF16),
            pltpu.VMEM((EXPERTS, TOK), F32),
            dma((8,)),
            dma((4, CHIPS, 4)),
            dma((CHIPS, 4)),
            dma((2,)),
            dma((2,)),
            dma((CHIPS,)),
            dma((CHIPS,)),
            dma((5,)),
            dma((5,)),
            dma,
            dma,
        ],
        compiler_params=pltpu.CompilerParams(
            collective_id=0, has_side_effects=True, vmem_limit_bytes=58 * 2**20
        ),
    )(g, ids, logits, h, w, r)


def on_device(out_grads, expert_ids, router_logits, hidden_acts, w_down, w_router):
    h = hidden_acts.reshape(CHIPS, CORES, MOST, FFW)
    scores, router, picked = exchange(
        out_grads[0], expert_ids[0], router_logits[0], h, w_down[0, 0], w_router[0]
    )
    score_grad = scores[:, :CORES].reshape(EXPERTS, TOK)
    picked_sum = jnp.sum(picked, axis=0, keepdims=True)
    mean_grad = jnp.sum(picked / picked_sum * score_grad, axis=0, keepdims=True)
    table = (score_grad - mean_grad) / picked_sum * picked * (1.0 - picked)
    last = lax.axis_index("pp") == lax.axis_size("pp") - 1
    table = jnp.where(last, 0.0, table).astype(BF16)
    result = lax.dot_general(table, router, (((0,), (0,)), ((), ())), preferred_element_type=F32)
    return result.astype(BF16)[None]


def solution(mesh):
    in_specs = (
        P("pp", "ep", None),
        P("pp", "ep", None),
        P("pp", "ep", None),
        P("pp", "ep", None, None),
        P("pp", "ep", None, None),
        P("pp", None, None),
    )
    out_specs = P("pp", "ep", None)
    return jax.shard_map(
        on_device, mesh=mesh, in_specs=in_specs, out_specs=out_specs, check_vma=False
    )
```

time: 235 us -> 134 us (0.57)
  waiting for transfers between devices: 158 us -> 0 us
  Pallas kernels: 0 us -> 126 us
  matrix products: 36.8 us -> 2.31 us
  starting transfers between devices: 25.5 us -> 0 us
  between operations: 13.5 us -> 0.01 us
  local copies, waits for them, and re-layouts: 0.01 us -> 3.7 us
    all_gather x1 -> x0, waiting for transfers between devices: 144 us -> none  [on_device(): upstream = lax.all_gather(out_grads[0], 'ep', axis=0)]
    pallas_call x0 -> x1, Pallas kernels: none -> 126 us  [exchange(): pl.pallas_call(kernel, out_shape=(jax.ShapeDtypeStruct((CHIPS, 8, TOK), F...]
    dot_general x4 -> x1, matrix products: 36.8 us -> 2.31 us  [on_device(): lax.dot_general(table, router, (((0,), (0,)), ((), ())), preferred_elemen...]
    all_to_all x2 -> x0, starting transfers between devices: 15 us -> none  [the longest x1 8.75 us: on_device(): lax.all_to_all(ranks.T, 'ep', split_axis=0, concat_axis=0, tiled=True)]
    ppermute x2 -> x0, starting transfers between devices: 10.5 us -> none  [passed_along(): return lax.ppermute(x, axis, pairs)]
    all_to_all x2 -> x0, waiting for transfers between devices: 7.6 us -> none  [the longest x1 7.6 us: on_device(): lax.all_to_all(scores, 'ep', split_axis=0, concat_axis=0, tiled=True)]
    ppermute x2 -> x0, waiting for transfers between devices: 5.21 us -> none  [passed_along(): return lax.ppermute(x, axis, pairs)]
    unnamed x4 -> x2, local copies, waits for them, and re-layouts: 0.01 us -> 2.85 us
  transfers between devices with their start and end apart: 5 -> 0, of which waited for: 3 -> 0; matrix products, arithmetic and copies ran while one was open for 16% -> 0% of each run, Pallas kernels for 0% -> 0%
where the time goes in v2:
time: 134 us; the launch traced here: 133 us
  Pallas kernels  126 us (94%)
  local copies, waits for them, and re-layouts  3.7 us (3%)
  matrix products  2.31 us (2%)
  other arithmetic  1.47 us (1%)
    pallas_call x1, Pallas kernels, exchange(): pl.pallas_call(kernel, out_shape=(jax.ShapeDtypeStruct((CHIPS, 8, TOK), F...  126 us
    unnamed x2, local copies, waits for them, and re-layouts  2.85 us

profile of v2, /device:TPU:8, one launch (start us, length us, event | category | flops | bytes accessed | tf_op | source)
XLA Modules:
  0.0 133.4 jit_solution(15710710939218897250)
XLA Ops:
  0.0 1.4 %copy.7 = s32[1,128,8]{2,1,0:T(8,128)} copy(s32[1,128,8]{1,2,0:T(8,128)} %param.7) | data formatting | bytes 8192 | tf_op args[1]
  1.4 1.4 %copy.8 = f32[1,128,32]{2,1,0:T(8,128)} copy(f32[1,128,32]{1,2,0:T(8,128)} %param.8) | data formatting | bytes 32768 | tf_op args[2]
  2.9 125.9 %shard_map.64 = (f32[16,8,128]{2,1,0:T(8,128)}, bf16[32,3584]{1,0:T(8,128)(2,1)}, f32[32,128]{1,0:T(8,128)}) custom-call(bf16[128,3584]{1,0:T(8,128)(2,1)} %bitcast.12, s32[128,8]{1,0:T(8,128)} %bitcast.14, f32[128,32]{1,0:T(8,128)} %bitcast.13, bf16[16,2,48,1024]{3,2,1,0:T(8,128)(2,1)} %bitcast.11, bf16[1024,3584]{1,0:T(8,128)(2,1)} %bitcast.10, ...), custom_call_target="tpu_custom_call" | custom-call | tf_op jit(solution)/shard_map/pallas_call | solution.py:466
  128.8 0.8 slice.3
  129.7 0.7 reduce_sum.18
  130.4 0.7 multiply_reduce_fusion
  131.1 2.3 %fusion = bf16[1,128,3584]{2,1,0:T(8,128)(2,1)} fusion(bf16[32,3584]{1,0:T(8,128)(2,1)} %get-tuple-element.10, f32[32,128]{1,0:T(8,128)} %get-tuple-element.9, f32[32,128]{1,0:T(8,128)S(1)} %bitcast.17, f32[128]{0:T(128)S(1)} %multiply_reduce_fusion, f32[128]{0:T(128)S(1)} %reduce_sum.18, pred[]{:T(512)S(6)} %eq.3), kind=kOutput, calls=%fused_computation.1 | convolution fusion | flops 29847552 | bytes 1180673 | tf_op jit(solution)/shard_map/dot_general | solution.py:519

commit v3 on v2

v3 whole, which is shorter than its diff:
```python
import functools

import jax
import jax.numpy as jnp
from jax import lax
from jax.experimental import pallas as pl
from jax.experimental.pallas import tpu as pltpu
from jax.sharding import PartitionSpec as P

MESH = pl.DeviceIdType.MESH
F32, BF16 = jnp.float32, jnp.bfloat16

X, Z, CORES = 4, 4, 2
CHIPS = X * Z
TOK, D, FFW, MOST, EXPERTS = 128, 3584, 1024, 48, 32
BOTH = CORES * MOST
WIDE, SLIM = 1408, 384
RANKS = 4
RANK_ROWS, RANK_LANES = 16, 256
QUARTER = D // X
HALF = D // 2

ORDER = (
    (
        12, 36, 100, 32, 8, 96, 97, 33, 9, 98, 34, 10, 99, 68, 108, 35, 44, 11, 20, 64, 40, 16, 65, 104, 17,
        106, 105, 42, 41, 18, 66, 76, 116, 67, 52, 107, 43, 19, 28, 48, 112, 24, 72, 49, 113, 25, 84, 73, 124, 60,
        114, 50, 26, 80, 56, 115, 51, 27, 74, 81, 75, 120, 122, 58, 123, 59, 121, 57, 92, 82, 83, 90, 91, 88, 89,
    ),
    (
        4, 20, 44, 108, 40, 0, 16, 104, 105, 41, 1, 17, 106, 42, 2, 18, 107, 76, 100, 116, 43, 36, 52, 3, 19,
        28, 98, 34, 72, 32, 99, 24, 35, 48, 96, 25, 73, 114, 112, 50, 26, 66, 115, 33, 67, 97, 51, 27, 113, 49,
        74, 68, 84, 75, 124, 122, 60, 58, 123, 59, 56, 120, 82, 83, 64, 57, 121, 65, 80, 81, 92, 90, 91, 89, 88,
    ),
    (
        12, 28, 52, 116, 48, 8, 24, 112, 113, 49, 9, 25, 114, 50, 10, 26, 115, 84, 108, 124, 51, 44, 60, 11, 27,
        4, 122, 58, 80, 40, 123, 0, 59, 56, 104, 1, 81, 106, 120, 42, 2, 90, 107, 41, 91, 105, 43, 3, 121, 57,
        82, 76, 92, 83, 100, 98, 36, 34, 99, 35, 32, 96, 74, 75, 72, 33, 97, 73, 88, 89, 68, 66, 67, 65, 64,
    ),
    (
        20, 60, 124, 56, 16, 120, 121, 57, 17, 122, 58, 18, 123, 92, 116, 59, 52, 19, 12, 88, 48, 8, 89, 112, 9,
        114, 113, 50, 49, 10, 90, 84, 108, 91, 44, 115, 51, 11, 4, 40, 104, 0, 80, 41, 105, 1, 76, 81, 100, 36,
        106, 42, 2, 72, 32, 107, 43, 3, 82, 73, 83, 96, 98, 34, 99, 35, 97, 33, 68, 74, 75, 66, 67, 64, 65,
    ),
)
EARLY = 14


def programme(z):
    late = [8 * z + p for p in range(4)] + [code for code in ORDER[z][:EARLY] if code % 8 != RANKS]
    steps = []
    for code in ORDER[z][EARLY:]:
        if late:
            steps.append(late.pop(0))
        steps.append(code + 128)
    left = {}
    for code in steps:
        left[code % 128 // 8] = left.get(code % 128 // 8, 0) + 1
    out = []
    for code in steps:
        shard = code % 128 // 8
        left[shard] -= 1
        out.append(code + (256 if left[shard] == 0 else 0))
    return out


STEPS = [programme(z) for z in range(Z)]
COUNT = max(map(len, STEPS))
IDLE = 5
STEPS = [steps + [IDLE] * (COUNT - len(steps)) for steps in STEPS]


def packed(codes):
    words = []
    for k in range(0, len(codes), 3):
        words.append(sum(code << (9 * j) for j, code in enumerate(codes[k : k + 3])))
    return words


def by_row(z, values):
    picked = jnp.int32(values[Z - 1])
    for row in range(Z - 1):
        picked = jnp.where(z == row, jnp.int32(values[row]), picked)
    return picked


def entry(words, i):
    place = lax.div(i, 3)
    while len(words) > 1:
        odd = lax.rem(place, 2) == 1
        halved = []
        for k in range(0, len(words), 2):
            more = k + 1 < len(words)
            halved.append(jnp.where(odd, words[k + 1], words[k]) if more else words[k])
        words, place = halved, lax.div(place, 2)
    turn = lax.rem(i, 3)
    scale = jnp.where(turn == 0, 1, jnp.where(turn == 1, 1 << 9, 1 << 18))
    return lax.rem(lax.div(words[0], scale), 512)


UP, DOWN, RIGHT, LEFT = range(4)


def goes(kind, x, z, xo, zo, piece):
    dx = lax.rem(xo - x + X, X)
    even = lax.rem(piece, 2) == 0
    odd = jnp.logical_not(even)
    up, down = (zo <= z) & (z < Z - 1), (zo >= z) & (z > 0)
    from_left, from_right = dx == X - 1, dx == 1
    here = dx == 0
    no = z < 0
    if kind == 2:
        return (here & up, here & down, here | from_left, here), (no,) * 4
    if kind == 0:
        whole = (here & up, here & down, here & even, here & odd)
        return whole, (no, no, (here & odd) | (from_left & even), (here & even) | (from_right & odd))
    row = zo == z
    across = row & (here | (from_left & even)), row & (here | (from_right & odd))
    return (up & (z != Z - 2), down & (z != 1), *across), (up & (z == Z - 2), down & (z == 1), no, no)


def arrives_whole(kind, x, z, xo, zo, piece):
    dx = lax.rem(xo - x + X, X)
    even = lax.rem(piece, 2) == 0
    if kind == 0:
        return (dx == 0) | ((dx == X - 1) & even) | ((dx == 1) & jnp.logical_not(even))
    return (zo == z) | ((z > 0) & (z < Z - 1))


def kernel(
    g_hbm, ids_hbm, logits_hbm, h_hbm, w_hbm, r_hbm,
    table_out, rn_out,
    held, ranks_of, wide_rows, slim_rows, prod, cross, hbuf, wbuf, acc, slot_acc, sent_scores,
    ids_v, logits_v, picked_v, st, rn, pk,
    load_sem, send_sem, recv_sem, cross_send, cross_recv,
    score_send, score_recv, r_send, r_recv, pk_send, pk_recv,
):
    sections = lax.axis_size("pp")
    s = lax.axis_index("pp")
    me = lax.axis_index("ep")
    core = lax.rem(me, CORES)
    chip = lax.div(me, CORES)
    x, z = lax.div(chip, Z), lax.rem(chip, Z)

    def at(xx, zz, cc=core):
        return (xx * Z + zz) * CORES + cc

    right, left = lax.rem(x + 1, X), lax.rem(x + X - 1, X)
    across = lax.rem(x + 2, X)
    sibling = (s, at(x, z, 1 - core))
    target = (
        (s, at(x, jnp.minimum(z + 1, Z - 1))),
        (s, at(x, jnp.maximum(z - 1, 0))),
        (s, at(right, z)),
        (s, at(left, z)),
    )
    opposite = (s, at(across, z))
    below = jnp.maximum(s - 1, 0)
    above = jnp.minimum(s + 1, sections - 1)

    def load(k, src, dst):
        return pltpu.make_async_copy(src, dst, load_sem.at[k])

    loads = [
        load(0, g_hbm, held.at[chip]),
        load(1, ids_hbm, ids_v),
        load(2, logits_hbm, logits_v),
        load(3, h_hbm.at[:, 1 - core], hbuf.at[0]),
        load(4, w_hbm.at[:, pl.ds(0, HALF)], wbuf.at[:, pl.ds(0, HALF)]),
        load(5, w_hbm.at[:, pl.ds(HALF, HALF)], wbuf.at[:, pl.ds(HALF, HALF)]),
        load(6, h_hbm.at[:, core], hbuf.at[1]),
    ]
    for copy in loads:
        copy.start()

    barrier = pltpu.get_barrier_semaphore()

    def greet(device):
        pl.semaphore_signal(barrier, inc=1, device_id=device, device_id_type=MESH)

    for device in (target[2], target[3], opposite, sibling):
        greet(device)

    @pl.when(z < Z - 1)
    def _():
        greet(target[0])

    @pl.when(z > 0)
    def _():
        greet(target[1])

    @pl.when(s < sections - 1)
    def _():
        @pl.loop(0, CHIPS)
        def _(q):
            greet((above, q * CORES + core))

    loads[1].wait()
    loads[2].wait()
    experts = lax.broadcasted_iota(jnp.int32, (EXPERTS, TOK), 0)
    ids = ids_v[...]
    named = jnp.zeros((EXPERTS, TOK), F32)
    for k in range(ids.shape[0]):
        named = named + (ids[k : k + 1] == experts).astype(F32)
    upper = (
        lax.broadcasted_iota(jnp.int32, (TOK, TOK), 0)
        < lax.broadcasted_iota(jnp.int32, (TOK, TOK), 1)
    ).astype(BF16)
    before = jnp.dot(named.astype(BF16), upper, preferred_element_type=F32)
    ranks = jnp.where(named > 0, before, -1.0).astype(BF16)
    ranks_of[chip] = jnp.concatenate([ranks[:RANK_ROWS], ranks[RANK_ROWS:]], axis=1)
    affinity = 1.0 / (1.0 + jnp.exp(-logits_v[...]))
    picked_v[...] = jnp.where(named > 0, affinity, 0.0)

    calls = 4 + (z < Z - 1).astype(jnp.int32) + (z > 0).astype(jnp.int32)
    calls = calls + CHIPS * (s > 0).astype(jnp.int32)
    pl.semaphore_wait(barrier, calls)

    def remote(src, dst, send, recv, device):
        return pltpu.make_async_remote_copy(
            src_ref=src, dst_ref=dst, send_sem=send, recv_sem=recv,
            device_id=device, device_id_type=MESH,
        )

    def lanes_of(kind, piece):
        if kind == 0:
            return pl.ds(pl.multiple_of(piece * WIDE, 128), WIDE)
        return pl.ds(pl.multiple_of(2 * WIDE + (piece - 2) * SLIM, 128), SLIM)

    def whole_ref(q, kind, piece):
        if kind == 2:
            return ranks_of.at[q]
        return held.at[q, :, lanes_of(kind, piece)]

    def rows_ref(q, kind, piece):
        if kind == 0:
            own = lax.div(q, Z) == x
            return wide_rows.at[piece, 2 * lax.rem(q, Z) + jnp.where(own, 0, 1)]
        return slim_rows.at[piece - 2, q]

    def passing(way, q, kind, piece):
        ref = whole_ref(q, kind, piece)
        return remote(ref, ref, send_sem.at[way, q, piece], recv_sem.at[q, piece], target[way])

    def passing_rows(way, q, kind, piece):
        return remote(
            rows_ref(q, kind, piece),
            held.at[q, pl.ds(0, BOTH), lanes_of(kind, piece)],
            send_sem.at[way, q, piece], recv_sem.at[q, piece], target[way],
        )

    def chosen_rows(q, of):
        group = pl.ds(pl.multiple_of(lax.div(of * CORES, RANK_ROWS) * TOK, TOK), TOK)
        table = ranks_of[q, :, group].astype(F32)
        line = lax.broadcasted_iota(jnp.int32, (RANK_ROWS, TOK), 0)
        slot = lax.broadcasted_iota(jnp.int32, (MOST, TOK), 0).astype(F32)
        first = lax.rem(of * CORES, RANK_ROWS)
        hits = []
        for e in range(CORES):
            rank = jnp.sum(jnp.where(line == first + e, table, 0.0), axis=0, keepdims=True)
            hits.append(slot == rank)
        return hits

    neighbours = (chip + 1, chip - 1, right * Z + z, left * Z + z)

    def pass_on(q, kind, piece):
        whole, some = goes(kind, x, z, lax.div(q, Z), lax.rem(q, Z), piece)
        for way in range(4):

            @pl.when(whole[way])
            def _(way=way):
                passing(way, q, kind, piece).start()

        if kind == 2:
            return
        of, any_rows = chip, z < 0
        for way in range(4):
            of = jnp.where(some[way], neighbours[way], of)
            any_rows = any_rows | some[way]

        @pl.when(any_rows)
        def _():
            pick = jnp.concatenate([hit.astype(F32) for hit in chosen_rows(q, of)], axis=0)
            rows = jnp.dot(
                pick.astype(BF16), held[q, :, lanes_of(kind, piece)], preferred_element_type=F32
            )
            rows_ref(q, kind, piece)[...] = rows.astype(BF16)
            for way in range(4):

                @pl.when(some[way])
                def _(way=way):
                    passing_rows(way, q, kind, piece).start()

    rows = pl.ds(pl.multiple_of(core * RANK_ROWS, RANK_ROWS), RANK_ROWS)

    def quarter(xx):
        return pl.ds(pl.multiple_of(xx * QUARTER, 128), QUARTER)

    router_down = remote(
        r_hbm.at[rows, quarter(x)], rn.at[rows, quarter(x)], r_send.at[0], r_recv.at[0], (below, me)
    )

    @pl.when(s > 0)
    def _():
        router_down.start()

    pass_on(chip, 2, jnp.int32(RANKS))
    loads[0].wait()
    for piece in range(4):
        pass_on(chip, piece // 2, jnp.int32(piece))
    picked_down = remote(picked_v, pk, pk_send, pk_recv, (below, me))

    @pl.when(s > 0)
    def _():
        picked_down.start()

    steps = [by_row(z, words) for words in zip(*map(packed, STEPS))]
    early = [by_row(z, words) for words in zip(*(packed(row[:EARLY]) for row in ORDER))]

    def outputs(which, half, store):
        lhs = hbuf[which].reshape(CHIPS * MOST, FFW)

        @pl.loop(0, HALF // 256)
        def _(t):
            cols = pl.ds(pl.multiple_of(half * HALF + t * 256, 256), 256)
            out = jnp.dot(lhs, wbuf[:, cols], preferred_element_type=F32)
            store(cols, out.astype(BF16).reshape(CHIPS, MOST, 256))

    def store_cross(cols, value):
        cross[:, :, cols] = value

    def store_own(cols, value):
        prod[:, core, :, cols] = value

    def crossing(half):
        cols = pl.ds(half * HALF, HALF)
        return remote(
            cross.at[:, :, cols], prod.at[:, core, :, cols],
            cross_send.at[half], cross_recv.at[half], sibling,
        )

    loads[3].wait()
    for half in range(2):
        loads[4 + half].wait()
        outputs(0, half, store_cross)
        crossing(half).start()
    loads[6].wait()
    for half in range(2):
        outputs(1, half, store_own)

    def take(q, kind, piece):
        if kind == 2:
            passing(RIGHT, q, kind, piece).wait_recv()
        else:
            full = arrives_whole(kind, x, z, lax.div(q, Z), lax.rem(q, Z), piece)

            @pl.when(full)
            def _():
                passing(RIGHT, q, kind, piece).wait_recv()

            @pl.when(jnp.logical_not(full))
            def _():
                passing_rows(RIGHT, q, kind, piece).wait_recv()

        pass_on(q, kind, piece)

    def decode(code):
        shard = lax.rem(code, 128)
        xo = lax.rem(x + lax.div(shard, 32), X)
        zo = lax.rem(lax.div(shard, 8), Z)
        return xo * Z + zo, lax.rem(shard, 8)

    def by_kind(piece, act):
        for kind, cond in ((0, piece < 2), (1, (piece == 2) | (piece == 3)), (2, piece == RANKS)):

            @pl.when(cond)
            def _(kind=kind):
                act(kind, piece)

    @pl.loop(0, EARLY)
    def _(i):
        q, piece = decode(entry(early, i))
        by_kind(piece, functools.partial(take, q))

    def spread(k, device):
        ref = rn.at[rows, quarter(x)]
        return remote(ref, ref, r_send.at[1 + k], r_recv.at[1 + k], device)

    def came(k, xx):
        ref = rn.at[rows, quarter(xx)]
        return remote(ref, ref, r_send.at[1 + k], r_recv.at[1 + k], target[2])

    spreads = [spread(0, target[2]), spread(1, target[3]), spread(2, opposite)]
    own_rows = remote(rn.at[rows], rn.at[rows], r_send.at[4], r_recv.at[4], sibling)
    other = pl.ds(pl.multiple_of((1 - core) * RANK_ROWS, RANK_ROWS), RANK_ROWS)
    other_rows = remote(rn.at[other], rn.at[other], r_send.at[4], r_recv.at[4], sibling)

    @pl.when(s < sections - 1)
    def _():
        router_down.wait_recv()
        for copy in spreads:
            copy.start()

    for half in range(2):
        crossing(half).wait_recv()
    acc[...] = jnp.zeros_like(acc)
    slot_acc[...] = jnp.zeros_like(slot_acc)

    def score_copy(q):
        return remote(
            sent_scores.at[q], st.at[chip], score_send.at[q], score_recv.at[chip],
            (below, q * CORES + core),
        )

    def score(q, kind, piece):
        cols = lanes_of(kind, piece)
        width = (WIDE, SLIM)[kind]
        full = arrives_whole(kind, x, z, lax.div(q, Z), lax.rem(q, Z), piece)

        @pl.when(full)
        def _():
            acc[q] += lax.dot_general(
                prod[q, :, :, cols].reshape(BOTH, width), held[q, :, cols],
                (((1,), (1,)), ((), ())), preferred_element_type=F32,
            )

        @pl.when(jnp.logical_not(full))
        def _():
            terms = prod[q, :, :, cols].reshape(BOTH, width).astype(F32)
            terms = terms * held[q, :BOTH, cols].astype(F32)
            total = slot_acc[q]
            for k in range(0, width, TOK):
                total = total + terms[:, k : k + TOK]
            slot_acc[q] = total

    def finish(q):
        total = acc[q] + jnp.sum(slot_acc[q], axis=1, keepdims=True)
        tile = lax.broadcasted_iota(jnp.int32, (8, TOK), 0)
        result = jnp.zeros((8, TOK), F32)
        for e, hit in enumerate(chosen_rows(q, chip)):
            part = total[e * MOST : (e + 1) * MOST]
            row = jnp.sum(jnp.where(hit, part, 0.0), axis=0, keepdims=True)
            result = jnp.where(tile == e, row, result)
        sent_scores[q] = result

        @pl.when(s > 0)
        def _():
            score_copy(q).start()

    @pl.loop(0, COUNT)
    def _(i):
        code = entry(steps, i)
        q, piece = decode(code)
        new = lax.rem(lax.div(code, 128), 2) == 1

        def step(kind, which):
            @pl.when(new)
            def _():
                take(q, kind, which)

            if kind < 2:
                score(q, kind, which)

        by_kind(piece, step)

        @pl.when(code >= 256)
        def _():
            finish(q)

        @pl.when((i == COUNT // 2) & (s < sections - 1))
        def _():
            came(0, left).wait_recv()
            came(1, right).wait_recv()
            came(2, across).wait_recv()
            own_rows.start()

    @pl.when(s < sections - 1)
    def _():
        other_rows.wait_recv()
        rn_out[...] = rn[...]
        picked_down.wait_recv()

        @pl.loop(0, CHIPS)
        def _(q):
            remote(
                sent_scores.at[q], st.at[q], score_send.at[q], score_recv.at[q], (below, me)
            ).wait_recv()

        picked = pk[...]
        score_grad = jnp.concatenate([st[q, :CORES] for q in range(CHIPS)], axis=0)
        picked_sum = jnp.sum(picked, axis=0, keepdims=True)
        mean_grad = jnp.sum(picked / picked_sum * score_grad, axis=0, keepdims=True)
        table = (score_grad - mean_grad) / picked_sum * picked * (1.0 - picked)
        square = jnp.concatenate([table, jnp.zeros((TOK - EXPERTS, TOK), F32)], axis=0)
        table_out[...] = square.T[:, :EXPERTS].astype(BF16)

    @pl.when(s == sections - 1)
    def _():
        rn_out[...] = jnp.zeros_like(rn_out)
        table_out[...] = jnp.zeros_like(table_out)

    for half in range(2):
        crossing(half).wait_send()

    @pl.when(s < sections - 1)
    def _():
        for copy in spreads:
            copy.wait_send()
        own_rows.wait_send()

    @pl.when(s > 0)
    def _():
        router_down.wait_send()
        picked_down.wait_send()

        @pl.loop(0, CHIPS)
        def _(q):
            score_copy(q).wait_send()

    @pl.loop(0, CHIPS)
    def _(q):
        for kind, pieces in ((0, (0, 1)), (1, (2, 3)), (2, (RANKS,))):
            for piece in pieces:
                whole, some = goes(kind, x, z, lax.div(q, Z), lax.rem(q, Z), jnp.int32(piece))
                for way in range(4):

                    @pl.when(whole[way])
                    def _(kind=kind, piece=piece, way=way):
                        passing(way, q, kind, jnp.int32(piece)).wait_send()

                    if kind < 2:

                        @pl.when(some[way])
                        def _(kind=kind, piece=piece, way=way):
                            passing_rows(way, q, kind, jnp.int32(piece)).wait_send()


def exchange(g, ids, logits, h, w, r):
    vmem = pl.BlockSpec(memory_space=pltpu.VMEM)
    dma = pltpu.SemaphoreType.DMA
    return pl.pallas_call(
        kernel,
        out_shape=(
            jax.ShapeDtypeStruct((TOK, EXPERTS), BF16),
            jax.ShapeDtypeStruct((EXPERTS, D), BF16),
        ),
        in_specs=[pl.BlockSpec(memory_space=pl.ANY)] * 6,
        out_specs=(vmem,) * 2,
        scratch_shapes=[
            pltpu.VMEM((CHIPS, TOK, D), BF16),
            pltpu.VMEM((CHIPS, RANK_ROWS, RANK_LANES), BF16),
            pltpu.VMEM((2, 2 * Z, BOTH, WIDE), BF16),
            pltpu.VMEM((2, CHIPS, BOTH, SLIM), BF16),
            pltpu.VMEM((CHIPS, CORES, MOST, D), BF16),
            pltpu.VMEM((CHIPS, MOST, D), BF16),
            pltpu.VMEM((CORES, CHIPS, MOST, FFW), BF16),
            pltpu.VMEM((FFW, D), BF16),
            pltpu.VMEM((CHIPS, BOTH, TOK), F32),
            pltpu.VMEM((CHIPS, BOTH, TOK), F32),
            pltpu.VMEM((CHIPS, 8, TOK), F32),
            pltpu.VMEM(ids.shape, jnp.int32),
            pltpu.VMEM(logits.shape, F32),
            pltpu.VMEM((EXPERTS, TOK), F32),
            pltpu.VMEM((CHIPS, 8, TOK), F32),
            pltpu.VMEM((EXPERTS, D), BF16),
            pltpu.VMEM((EXPERTS, TOK), F32),
            dma((7,)),
            dma((4, CHIPS, 5)),
            dma((CHIPS, 5)),
            dma((2,)),
            dma((2,)),
            dma((CHIPS,)),
            dma((CHIPS,)),
            dma((5,)),
            dma((5,)),
            dma,
            dma,
        ],
        compiler_params=pltpu.CompilerParams(
            collective_id=0, has_side_effects=True, vmem_limit_bytes=58 * 2**20
        ),
    )(g, ids, logits, h, w, r)


def on_device(out_grads, expert_ids, router_logits, hidden_acts, w_down, w_router):
    h = hidden_acts.reshape(CHIPS, CORES, MOST, FFW)
    table, router = exchange(
        out_grads[0], expert_ids[0].T, router_logits[0].T, h, w_down[0, 0], w_router[0]
    )
    return jnp.dot(table, router, preferred_element_type=F32).astype(BF16)[None]


def solution(mesh):
    in_specs = (
        P("pp", "ep", None),
        P("pp", "ep", None),
        P("pp", "ep", None),
        P("pp", "ep", None, None),
        P("pp", "ep", None, None),
        P("pp", None, None),
    )
    out_specs = P("pp", "ep", None)
    return jax.shard_map(
        on_device, mesh=mesh, in_specs=in_specs, out_specs=out_specs, check_vma=False
    )
```

time: 134 us -> 112 us (0.84)
  Pallas kernels: 126 us -> 110 us
  local copies, waits for them, and re-layouts: 3.7 us -> 0 us
  other arithmetic: 1.47 us -> 0 us
    pallas_call x1, Pallas kernels: 126 us -> 110 us  [exchange(): pl.pallas_call(kernel, out_shape=(jax.ShapeDtypeStruct((TOK, EXPERTS), BF...]
    unnamed x2 -> x0, local copies, waits for them, and re-layouts: 2.85 us -> none
    reduce_sum x2 -> x0, other arithmetic: 1.47 us -> none  [the longest x1 0.74 us: on_device(): mean_grad = jnp.sum(picked / picked_sum * score_grad, axis=0, keepdims=True)]
where the time goes in v3:
time: 112 us
  Pallas kernels  110 us (98%)
  matrix products  2.26 us (2%)
    pallas_call x1, Pallas kernels, exchange(): pl.pallas_call(kernel, out_shape=(jax.ShapeDtypeStruct((TOK, EXPERTS), BF...  110 us
    dot_general x1, matrix products, on_device(): return jnp.dot(table, router, preferred_element_type=F32).astype(BF16)[None]  2.26 us

profile of v3, /device:TPU:8, one launch (start us, length us, event | category | flops | bytes accessed | tf_op | source)
XLA Modules:
  0.0 112.1 jit_solution(3615818257396590379)
XLA Ops:
  0.0 109.9 %shard_map.64 = (bf16[128,32]{1,0:T(8,128)(2,1)}, bf16[32,3584]{1,0:T(8,128)(2,1)}) custom-call(bf16[128,3584]{1,0:T(8,128)(2,1)} %bitcast.16, s32[8,128]{1,0:T(8,128)} %bitcast.19, f32[32,128]{1,0:T(8,128)} %bitcast.18, bf16[16,2,48,1024]{3,2,1,0:T(8,128)(2,1)} %bitcast.15, bf16[1024,3584]{1,0:T(8,128)(2,1)} %bitcast.14, bf16[32,3584]{1,0:T(8,128)(2,1)} %bitcast.17), custom_call_target="tpu_custom_call" | custom-call | tf_op jit(solution)/shard_map/pallas_call | solution.py:540
  109.9 2.3 %fusion = bf16[1,128,3584]{2,1,0:T(8,128)(2,1)} fusion(bf16[128,32]{1,0:T(8,128)(2,1)} %get-tuple-element.7, bf16[32,3584]{1,0:T(8,128)(2,1)} %get-tuple-element.8), kind=kOutput, calls=%fused_computation.1 | convolution fusion | flops 29818880 | bytes 1155072 | tf_op jit(solution)/shard_map/dot_general | solution.py:589

commit v4 on v3

--- a/solution.py
+++ b/solution.py
@@ -14,7 +14,8 @@
 CHIPS = X * Z
 TOK, D, FFW, MOST, EXPERTS = 128, 3584, 1024, 48, 32
 BOTH = CORES * MOST
-WIDE, SLIM = 1408, 384
+WIDTH = (1408, 1408, 384, 384)
+OFFSET = (0, 1408, 2816, 3200)
 RANKS = 4
 RANK_ROWS, RANK_LANES = 16, 256
 QUARTER = D // X
@@ -98,32 +99,53 @@
 
 
 UP, DOWN, RIGHT, LEFT = range(4)
-
-
-def goes(kind, x, z, xo, zo, piece):
-    dx = lax.rem(xo - x + X, X)
-    even = lax.rem(piece, 2) == 0
-    odd = jnp.logical_not(even)
+WHOLE, ROWS = range(2)
+
+
+def rem(a, b):
+    return a % b if isinstance(a, int) else lax.rem(a, b)
+
+
+def goes(piece, x, z, xo, zo):
+    dx = rem(xo - x + X, X)
+    even = piece % 2 == 0
     up, down = (zo <= z) & (z < Z - 1), (zo >= z) & (z > 0)
-    from_left, from_right = dx == X - 1, dx == 1
     here = dx == 0
+    beside = dx == (X - 1 if even else 1)
     no = z < 0
-    if kind == 2:
-        return (here & up, here & down, here | from_left, here), (no,) * 4
-    if kind == 0:
-        whole = (here & up, here & down, here & even, here & odd)
-        return whole, (no, no, (here & odd) | (from_left & even), (here & even) | (from_right & odd))
+    if piece == RANKS:
+        return (here & up, here & down, here | beside, here), (no,) * 4
+    if piece < 2:
+        if even:
+            return (here & up, here & down, here, no), (no, no, beside, here)
+        return (here & up, here & down, no, here), (no, no, here, beside)
     row = zo == z
-    across = row & (here | (from_left & even)), row & (here | (from_right & odd))
+    across = (row & (here | beside), row & here)
+    if not even:
+        across = across[::-1]
     return (up & (z != Z - 2), down & (z != 1), *across), (up & (z == Z - 2), down & (z == 1), no, no)
 
 
-def arrives_whole(kind, x, z, xo, zo, piece):
-    dx = lax.rem(xo - x + X, X)
-    even = lax.rem(piece, 2) == 0
-    if kind == 0:
-        return (dx == 0) | ((dx == X - 1) & even) | ((dx == 1) & jnp.logical_not(even))
+def arrives_whole(piece, x, z, xo, zo):
+    dx = rem(xo - x + X, X)
+    if piece < 2:
+        return (dx == 0) | (dx == (X - 1 if piece == 0 else 1))
     return (zo == z) | ((z > 0) & (z < Z - 1))
+
+
+def sends(row):
+    count = {}
+    for q in range(CHIPS):
+        for piece in range(5):
+            for form, ways in enumerate(goes(piece, 0, row, q // Z, q % Z)):
+                for way in range(4):
+                    if ways[way]:
+                        count[way, piece, form] = count.get((way, piece, form), 0) + 1
+    return count
+
+
+SENDS = [sends(row) for row in range(Z)]
+GROUPS = sorted(set().union(*SENDS))
 
 
 def kernel(
@@ -221,31 +243,30 @@
             device_id=device, device_id_type=MESH,
         )
 
-    def lanes_of(kind, piece):
-        if kind == 0:
-            return pl.ds(pl.multiple_of(piece * WIDE, 128), WIDE)
-        return pl.ds(pl.multiple_of(2 * WIDE + (piece - 2) * SLIM, 128), SLIM)
-
-    def whole_ref(q, kind, piece):
-        if kind == 2:
+    def lanes_of(piece):
+        return pl.ds(OFFSET[piece], WIDTH[piece])
+
+    def whole_ref(q, piece):
+        if piece == RANKS:
             return ranks_of.at[q]
-        return held.at[q, :, lanes_of(kind, piece)]
-
-    def rows_ref(q, kind, piece):
-        if kind == 0:
+        return held.at[q, :, lanes_of(piece)]
+
+    def rows_ref(q, piece):
+        if piece < 2:
             own = lax.div(q, Z) == x
-            return wide_rows.at[piece, 2 * lax.rem(q, Z) + jnp.where(own, 0, 1)]
-        return slim_rows.at[piece - 2, q]
-
-    def passing(way, q, kind, piece):
-        ref = whole_ref(q, kind, piece)
-        return remote(ref, ref, send_sem.at[way, q, piece], recv_sem.at[q, piece], target[way])
-
-    def passing_rows(way, q, kind, piece):
+            place = 2 * lax.rem(q, Z) + jnp.where(own, 0, 1)
+            return wide_rows.at[place, :, lanes_of(piece)]
+        return slim_rows.at[q, :, pl.ds(OFFSET[piece] - OFFSET[2], WIDTH[piece])]
+
+    def passing(way, q, piece):
+        ref = whole_ref(q, piece)
+        sent = send_sem.at[GROUPS.index((way, piece, WHOLE))]
+        return remote(ref, ref, sent, recv_sem.at[q, piece], target[way])
+
+    def passing_rows(way, q, piece):
         return remote(
-            rows_ref(q, kind, piece),
-            held.at[q, pl.ds(0, BOTH), lanes_of(kind, piece)],
-            send_sem.at[way, q, piece], recv_sem.at[q, piece], target[way],
+            rows_ref(q, piece), held.at[q, pl.ds(0, BOTH), lanes_of(piece)],
+            send_sem.at[GROUPS.index((way, piece, ROWS))], recv_sem.at[q, piece], target[way],
         )
 
     def chosen_rows(q, of):
@@ -262,15 +283,16 @@
 
     neighbours = (chip + 1, chip - 1, right * Z + z, left * Z + z)
 
-    def pass_on(q, kind, piece):
-        whole, some = goes(kind, x, z, lax.div(q, Z), lax.rem(q, Z), piece)
+    def pass_on(q, piece):
+        whole, some = goes(piece, x, z, lax.div(q, Z), lax.rem(q, Z))
         for way in range(4):
-
-            @pl.when(whole[way])
-            def _(way=way):
-                passing(way, q, kind, piece).start()
-
-        if kind == 2:
+            if (way, piece, WHOLE) in GROUPS:
+
+                @pl.when(whole[way])
+                def _(way=way):
+                    passing(way, q, piece).start()
+
+        if piece == RANKS:
             return
         of, any_rows = chip, z < 0
         for way in range(4):
@@ -281,14 +303,15 @@
         def _():
             pick = jnp.concatenate([hit.astype(F32) for hit in chosen_rows(q, of)], axis=0)
             rows = jnp.dot(
-                pick.astype(BF16), held[q, :, lanes_of(kind, piece)], preferred_element_type=F32
+                pick.astype(BF16), held[q, :, lanes_of(piece)], preferred_element_type=F32
             )
-            rows_ref(q, kind, piece)[...] = rows.astype(BF16)
+            rows_ref(q, piece)[...] = rows.astype(BF16)
             for way in range(4):
-
-                @pl.when(some[way])
-                def _(way=way):
-                    passing_rows(way, q, kind, piece).start()
+                if (way, piece, ROWS) in GROUPS:
+
+                    @pl.when(some[way])
+                    def _(way=way):
+                        passing_rows(way, q, piece).start()
 
     rows = pl.ds(pl.multiple_of(core * RANK_ROWS, RANK_ROWS), RANK_ROWS)
 
@@ -303,10 +326,10 @@
     def _():
         router_down.start()
 
-    pass_on(chip, 2, jnp.int32(RANKS))
+    pass_on(chip, RANKS)
     loads[0].wait()
     for piece in range(4):
-        pass_on(chip, piece // 2, jnp.int32(piece))
+        pass_on(chip, piece)
     picked_down = remote(picked_v, pk, pk_send, pk_recv, (below, me))
 
     @pl.when(s > 0)
@@ -347,21 +370,24 @@
     for half in range(2):
         outputs(1, half, store_own)
 
-    def take(q, kind, piece):
-        if kind == 2:
-            passing(RIGHT, q, kind, piece).wait_recv()
+    def arrived(q, piece, ref):
+        remote(ref, ref, send_sem.at[0], recv_sem.at[q, piece], target[RIGHT]).wait_recv()
+
+    def take(q, piece):
+        if piece == RANKS:
+            arrived(q, piece, ranks_of.at[q])
         else:
-            full = arrives_whole(kind, x, z, lax.div(q, Z), lax.rem(q, Z), piece)
+            full = arrives_whole(piece, x, z, lax.div(q, Z), lax.rem(q, Z))
 
             @pl.when(full)
             def _():
-                passing(RIGHT, q, kind, piece).wait_recv()
+                arrived(q, piece, held.at[q, :, lanes_of(piece)])
 
             @pl.when(jnp.logical_not(full))
             def _():
-                passing_rows(RIGHT, q, kind, piece).wait_recv()
-
-        pass_on(q, kind, piece)
+                arrived(q, piece, held.at[q, pl.ds(0, BOTH), lanes_of(piece)])
+
+        pass_on(q, piece)
 
     def decode(code):
         shard = lax.rem(code, 128)
@@ -369,17 +395,17 @@
         zo = lax.rem(lax.div(shard, 8), Z)
         return xo * Z + zo, lax.rem(shard, 8)
 
-    def by_kind(piece, act):
-        for kind, cond in ((0, piece < 2), (1, (piece == 2) | (piece == 3)), (2, piece == RANKS)):
-
-            @pl.when(cond)
-            def _(kind=kind):
-                act(kind, piece)
+    def by_piece(piece, act):
+        for k in range(5):
+
+            @pl.when(piece == k)
+            def _(k=k):
+                act(k)
 
     @pl.loop(0, EARLY)
     def _(i):
         q, piece = decode(entry(early, i))
-        by_kind(piece, functools.partial(take, q))
+        by_piece(piece, functools.partial(take, q))
 
     def spread(k, device):
         ref = rn.at[rows, quarter(x)]
@@ -407,14 +433,13 @@
 
     def score_copy(q):
         return remote(
-            sent_scores.at[q], st.at[chip], score_send.at[q], score_recv.at[chip],
+            sent_scores.at[q], st.at[chip], score_send, score_recv,
             (below, q * CORES + core),
         )
 
-    def score(q, kind, piece):
-        cols = lanes_of(kind, piece)
-        width = (WIDE, SLIM)[kind]
-        full = arrives_whole(kind, x, z, lax.div(q, Z), lax.rem(q, Z), piece)
+    def score(q, piece):
+        cols, width = lanes_of(piece), WIDTH[piece]
+        full = arrives_whole(piece, x, z, lax.div(q, Z), lax.rem(q, Z))
 
         @pl.when(full)
         def _():
@@ -434,13 +459,11 @@
 
     def finish(q):
         total = acc[q] + jnp.sum(slot_acc[q], axis=1, keepdims=True)
-        tile = lax.broadcasted_iota(jnp.int32, (8, TOK), 0)
-        result = jnp.zeros((8, TOK), F32)
+        lines = []
         for e, hit in enumerate(chosen_rows(q, chip)):
             part = total[e * MOST : (e + 1) * MOST]
-            row = jnp.sum(jnp.where(hit, part, 0.0), axis=0, keepdims=True)
-            result = jnp.where(tile == e, row, result)
-        sent_scores[q] = result
+            lines.append(jnp.sum(jnp.where(hit, part, 0.0), axis=0, keepdims=True))
+        sent_scores[q] = jnp.concatenate(lines, axis=0)
 
         @pl.when(s > 0)
         def _():
@@ -452,15 +475,15 @@
         q, piece = decode(code)
         new = lax.rem(lax.div(code, 128), 2) == 1
 
-        def step(kind, which):
+        def step(k):
             @pl.when(new)
             def _():
-                take(q, kind, which)
-
-            if kind < 2:
-                score(q, kind, which)
-
-        by_kind(piece, step)
+                take(q, k)
+
+            if k != RANKS:
+                score(q, k)
+
+        by_piece(piece, step)
 
         @pl.when(code >= 256)
         def _():
@@ -479,14 +502,9 @@
         rn_out[...] = rn[...]
         picked_down.wait_recv()
 
-        @pl.loop(0, CHIPS)
-        def _(q):
-            remote(
-                sent_scores.at[q], st.at[q], score_send.at[q], score_recv.at[q], (below, me)
-            ).wait_recv()
-
+        remote(sent_scores, st, score_send, score_recv, (below, me)).wait_recv()
         picked = pk[...]
-        score_grad = jnp.concatenate([st[q, :CORES] for q in range(CHIPS)], axis=0)
+        score_grad = jnp.concatenate([st[q] for q in range(CHIPS)], axis=0)
         picked_sum = jnp.sum(picked, axis=0, keepdims=True)
         mean_grad = jnp.sum(picked / picked_sum * score_grad, axis=0, keepdims=True)
         table = (score_grad - mean_grad) / picked_sum * picked * (1.0 - picked)
@@ -511,27 +529,19 @@
     def _():
         router_down.wait_send()
         picked_down.wait_send()
-
-        @pl.loop(0, CHIPS)
-        def _(q):
-            score_copy(q).wait_send()
-
-    @pl.loop(0, CHIPS)
-    def _(q):
-        for kind, pieces in ((0, (0, 1)), (1, (2, 3)), (2, (RANKS,))):
-            for piece in pieces:
-                whole, some = goes(kind, x, z, lax.div(q, Z), lax.rem(q, Z), jnp.int32(piece))
-                for way in range(4):
-
-                    @pl.when(whole[way])
-                    def _(kind=kind, piece=piece, way=way):
-                        passing(way, q, kind, jnp.int32(piece)).wait_send()
-
-                    if kind < 2:
-
-                        @pl.when(some[way])
-                        def _(kind=kind, piece=piece, way=way):
-                            passing_rows(way, q, kind, jnp.int32(piece)).wait_send()
+        remote(sent_scores, st, score_send, score_recv, (below, me)).wait_send()
+
+    for row in range(Z):
+
+        @pl.when(z == row)
+        def _(row=row):
+            for (way, piece, form), n in SENDS[row].items():
+                if piece == RANKS:
+                    ref = ranks_of.at[pl.ds(0, n)]
+                else:
+                    ref = held.at[pl.ds(0, n), pl.ds(0, (TOK, BOTH)[form]), lanes_of(piece)]
+                sent = send_sem.at[GROUPS.index((way, piece, form))]
+                remote(ref, ref, sent, recv_sem.at[0, 0], target[RIGHT]).wait_send()
 
 
 def exchange(g, ids, logits, h, w, r):
@@ -548,28 +558,28 @@
         scratch_shapes=[
             pltpu.VMEM((CHIPS, TOK, D), BF16),
             pltpu.VMEM((CHIPS, RANK_ROWS, RANK_LANES), BF16),
-            pltpu.VMEM((2, 2 * Z, BOTH, WIDE), BF16),
-            pltpu.VMEM((2, CHIPS, BOTH, SLIM), BF16),
+            pltpu.VMEM((2 * Z, BOTH, OFFSET[2]), BF16),
+            pltpu.VMEM((CHIPS, BOTH, D - OFFSET[2]), BF16),
             pltpu.VMEM((CHIPS, CORES, MOST, D), BF16),
             pltpu.VMEM((CHIPS, MOST, D), BF16),
             pltpu.VMEM((CORES, CHIPS, MOST, FFW), BF16),
             pltpu.VMEM((FFW, D), BF16),
             pltpu.VMEM((CHIPS, BOTH, TOK), F32),
             pltpu.VMEM((CHIPS, BOTH, TOK), F32),
-            pltpu.VMEM((CHIPS, 8, TOK), F32),
+            pltpu.VMEM((CHIPS, CORES, TOK), F32),
             pltpu.VMEM(ids.shape, jnp.int32),
             pltpu.VMEM(logits.shape, F32),
             pltpu.VMEM((EXPERTS, TOK), F32),
-            pltpu.VMEM((CHIPS, 8, TOK), F32),
+            pltpu.VMEM((CHIPS, CORES, TOK), F32),
             pltpu.VMEM((EXPERTS, D), BF16),
             pltpu.VMEM((EXPERTS, TOK), F32),
             dma((7,)),
-            dma((4, CHIPS, 5)),
+            dma((len(GROUPS),)),
             dma((CHIPS, 5)),
             dma((2,)),
             dma((2,)),
-            dma((CHIPS,)),
-            dma((CHIPS,)),
+            dma,
+            dma,
             dma((5,)),
             dma((5,)),
             dma,

time: 112 us -> 107 us (0.955)
  Pallas kernels: 110 us -> 105 us
    pallas_call x1, Pallas kernels: 110 us -> 105 us  [exchange(): pl.pallas_call(kernel, out_shape=(jax.ShapeDtypeStruct((TOK, EXPERTS), BF...]
where the time goes in v4:
time: 107 us
  Pallas kernels  105 us (98%)
  matrix products  2.26 us (2%)
    pallas_call x1, Pallas kernels, exchange(): pl.pallas_call(kernel, out_shape=(jax.ShapeDtypeStruct((TOK, EXPERTS), BF...  105 us
    dot_general x1, matrix products, on_device(): return jnp.dot(table, router, preferred_element_type=F32).astype(BF16)[None]  2.26 us

profile of v4, /device:TPU:8, one launch (start us, length us, event | category | flops | bytes accessed | tf_op | source)
XLA Modules:
  0.0 106.9 jit_solution(3984808071319686669)
XLA Ops:
  0.0 104.7 %shard_map.64 = (bf16[128,32]{1,0:T(8,128)(2,1)}, bf16[32,3584]{1,0:T(8,128)(2,1)}) custom-call(bf16[128,3584]{1,0:T(8,128)(2,1)} %bitcast.16, s32[8,128]{1,0:T(8,128)} %bitcast.19, f32[32,128]{1,0:T(8,128)} %bitcast.18, bf16[16,2,48,1024]{3,2,1,0:T(8,128)(2,1)} %bitcast.15, bf16[1024,3584]{1,0:T(8,128)(2,1)} %bitcast.14, bf16[32,3584]{1,0:T(8,128)(2,1)} %bitcast.17), custom_call_target="tpu_custom_call" | custom-call | tf_op jit(solution)/shard_map/pallas_call | solution.py:550
  104.7 2.3 %fusion = bf16[1,128,3584]{2,1,0:T(8,128)(2,1)} fusion(bf16[128,32]{1,0:T(8,128)(2,1)} %get-tuple-element.7, bf16[32,3584]{1,0:T(8,128)(2,1)} %get-tuple-element.8), kind=kOutput, calls=%fused_computation.1 | convolution fusion | flops 29818880 | bytes 1155072 | tf_op jit(solution)/shard_map/dot_general | solution.py:599

commit v5 on v4

--- a/solution.py
+++ b/solution.py
@@ -23,24 +23,24 @@
 
 ORDER = (
     (
-        12, 36, 100, 32, 8, 96, 97, 33, 9, 98, 34, 10, 99, 68, 108, 35, 44, 11, 20, 64, 40, 16, 65, 104, 17,
-        106, 105, 42, 41, 18, 66, 76, 116, 67, 52, 107, 43, 19, 28, 48, 112, 24, 72, 49, 113, 25, 84, 73, 124, 60,
-        114, 50, 26, 80, 56, 115, 51, 27, 74, 81, 75, 120, 122, 58, 123, 59, 121, 57, 92, 82, 83, 90, 91, 88, 89,
+        12, 36, 100, 11, 35, 99, 32, 8, 96, 33, 97, 9, 34, 98, 44, 68, 108, 10, 20, 67, 19, 43, 107, 40, 104,
+        16, 64, 65, 105, 17, 41, 66, 52, 76, 116, 42, 106, 18, 28, 48, 75, 72, 27, 51, 115, 49, 112, 24, 73, 60,
+        113, 84, 124, 81, 80, 25, 50, 114, 26, 56, 74, 120, 92, 59, 83, 123, 57, 58, 121, 122, 82, 91, 90, 88, 89,
     ),
     (
-        4, 20, 44, 108, 40, 0, 16, 104, 105, 41, 1, 17, 106, 42, 2, 18, 107, 76, 100, 116, 43, 36, 52, 3, 19,
-        28, 98, 34, 72, 32, 99, 24, 35, 48, 96, 25, 73, 114, 112, 50, 26, 66, 115, 33, 67, 97, 51, 27, 113, 49,
-        74, 68, 84, 75, 124, 122, 60, 58, 123, 59, 56, 120, 82, 83, 64, 57, 121, 65, 80, 81, 92, 90, 91, 89, 88,
+        4, 20, 44, 108, 3, 19, 43, 107, 40, 0, 16, 104, 41, 105, 1, 17, 42, 106, 36, 76, 52, 100, 116, 2, 18,
+        28, 75, 35, 27, 99, 72, 51, 32, 34, 115, 98, 67, 48, 96, 24, 73, 112, 25, 66, 50, 97, 33, 114, 26, 113,
+        49, 74, 60, 59, 68, 84, 83, 124, 123, 58, 122, 56, 64, 82, 57, 120, 65, 80, 81, 121, 92, 91, 90, 89, 88,
     ),
     (
-        12, 28, 52, 116, 48, 8, 24, 112, 113, 49, 9, 25, 114, 50, 10, 26, 115, 84, 108, 124, 51, 44, 60, 11, 27,
-        4, 122, 58, 80, 40, 123, 0, 59, 56, 104, 1, 81, 106, 120, 42, 2, 90, 107, 41, 91, 105, 43, 3, 121, 57,
-        82, 76, 92, 83, 100, 98, 36, 34, 99, 35, 32, 96, 74, 75, 72, 33, 97, 73, 88, 89, 68, 66, 67, 65, 64,
+        12, 28, 52, 116, 11, 27, 51, 115, 48, 8, 24, 112, 49, 113, 9, 25, 50, 114, 44, 84, 60, 108, 124, 10, 26,
+        4, 83, 59, 3, 123, 80, 43, 40, 58, 107, 122, 91, 56, 104, 0, 81, 120, 1, 90, 42, 105, 41, 106, 2, 121,
+        57, 82, 36, 35, 76, 75, 92, 100, 99, 34, 98, 32, 72, 74, 33, 96, 73, 88, 89, 97, 68, 67, 66, 65, 64,
     ),
     (
-        20, 60, 124, 56, 16, 120, 121, 57, 17, 122, 58, 18, 123, 92, 116, 59, 52, 19, 12, 88, 48, 8, 89, 112, 9,
-        114, 113, 50, 49, 10, 90, 84, 108, 91, 44, 115, 51, 11, 4, 40, 104, 0, 80, 41, 105, 1, 76, 81, 100, 36,
-        106, 42, 2, 72, 32, 107, 43, 3, 82, 73, 83, 96, 98, 34, 99, 35, 97, 33, 68, 74, 75, 66, 67, 64, 65,
+        20, 60, 124, 19, 59, 123, 56, 16, 120, 57, 121, 17, 58, 122, 52, 92, 116, 18, 12, 91, 11, 51, 115, 48, 112,
+        8, 88, 89, 113, 9, 49, 90, 44, 84, 108, 50, 114, 10, 4, 40, 83, 80, 3, 43, 107, 41, 104, 0, 81, 36,
+        105, 76, 100, 73, 72, 1, 42, 106, 2, 32, 82, 96, 68, 35, 75, 99, 33, 34, 97, 98, 74, 67, 66, 64, 65,
     ),
 )
 EARLY = 14
@@ -328,7 +328,7 @@
 
     pass_on(chip, RANKS)
     loads[0].wait()
-    for piece in range(4):
+    for piece in (3, 0, 1, 2):
         pass_on(chip, piece)
     picked_down = remote(picked_v, pk, pk_send, pk_recv, (below, me))
 
@@ -586,9 +586,9 @@
             dma,
         ],
         compiler_params=pltpu.CompilerParams(
-            collective_id=0, has_side_effects=True, vmem_limit_bytes=58 * 2**20
+            collective_id=0, has_side_effects=True, vmem_limit_bytes=52 * 2**20
         ),
-    )(g, ids, logits, h, w, r)
+    )(*(pltpu.with_memory_space_constraint(v, pltpu.HBM) for v in (g, ids, logits, h, w, r)))
 
 
 def on_device(out_grads, expert_ids, router_logits, hidden_acts, w_down, w_router):

time: 107 us -> 105 us (0.981)
  no operation moved by 1% of the time
where the time goes in v5:
time: 105 us
  Pallas kernels  104 us (99%)
  matrix products  1.3 us (1%)
    pallas_call x1, Pallas kernels, exchange(): pl.pallas_call(kernel, out_shape=(jax.ShapeDtypeStruct((TOK, EXPERTS), BF...  104 us

profile of v5, /device:TPU:8, one launch (start us, length us, event | category | flops | bytes accessed | tf_op | source)
XLA Modules:
  0.0 105.0 jit_solution(17825017378238237232)
XLA Ops:
  0.0 103.7 %shard_map.64 = (bf16[128,32]{1,0:T(8,128)(2,1)S(1)}, bf16[32,3584]{1,0:T(8,128)(2,1)S(1)}) custom-call(bf16[128,3584]{1,0:T(8,128)(2,1)} %bitcast.16, s32[8,128]{1,0:T(8,128)} %bitcast.19, f32[32,128]{1,0:T(8,128)} %bitcast.18, bf16[16,2,48,1024]{3,2,1,0:T(8,128)(2,1)} %bitcast.15, bf16[1024,3584]{1,0:T(8,128)(2,1)} %bitcast.14, bf16[32,3584]{1,0:T(8,128)(2,1)} %bitcast.17), custom_call_target="tpu_custom_call" | custom-call | tf_op jit(solution)/shard_map/pallas_call | solution.py:550
  103.7 1.3 %fusion = bf16[1,128,3584]{2,1,0:T(8,128)(2,1)} fusion(bf16[128,32]{1,0:T(8,128)(2,1)S(1)} %get-tuple-element.7, bf16[32,3584]{1,0:T(8,128)(2,1)S(1)} %get-tuple-element.8), kind=kOutput, calls=%fused_computation.1 | convolution fusion | flops 29818880 | bytes 1155072 | tf_op jit(solution)/shard_map/dot_general | solution.py:599

commit v6 on v5

--- a/solution.py
+++ b/solution.py
@@ -23,24 +23,24 @@
 
 ORDER = (
     (
-        12, 36, 100, 11, 35, 99, 32, 8, 96, 33, 97, 9, 34, 98, 44, 68, 108, 10, 20, 67, 19, 43, 107, 40, 104,
-        16, 64, 65, 105, 17, 41, 66, 52, 76, 116, 42, 106, 18, 28, 48, 75, 72, 27, 51, 115, 49, 112, 24, 73, 60,
-        113, 84, 124, 81, 80, 25, 50, 114, 26, 56, 74, 120, 92, 59, 83, 123, 57, 58, 121, 122, 82, 91, 90, 88, 89,
+        12, 36, 100, 10, 34, 98, 97, 9, 33, 32, 96, 8, 35, 99, 44, 108, 68, 11, 20, 66, 18, 42, 106, 105, 41,
+        17, 65, 64, 40, 16, 104, 67, 116, 76, 52, 43, 107, 19, 28, 113, 74, 73, 26, 50, 114, 112, 49, 25, 72, 124,
+        48, 84, 60, 80, 81, 24, 51, 115, 27, 121, 75, 57, 92, 82, 58, 122, 120, 59, 56, 123, 83, 90, 91, 89, 88,
     ),
     (
-        4, 20, 44, 108, 3, 19, 43, 107, 40, 0, 16, 104, 41, 105, 1, 17, 42, 106, 36, 76, 52, 100, 116, 2, 18,
-        28, 75, 35, 27, 99, 72, 51, 32, 34, 115, 98, 67, 48, 96, 24, 73, 112, 25, 66, 50, 97, 33, 114, 26, 113,
-        49, 74, 60, 59, 68, 84, 83, 124, 123, 58, 122, 56, 64, 82, 57, 120, 65, 80, 81, 121, 92, 91, 90, 89, 88,
+        4, 20, 44, 108, 2, 18, 42, 106, 105, 1, 17, 41, 40, 104, 0, 16, 43, 107, 36, 100, 52, 116, 76, 3, 19,
+        28, 74, 34, 26, 98, 50, 33, 97, 35, 114, 99, 66, 113, 49, 25, 72, 73, 24, 67, 51, 32, 96, 115, 27, 48,
+        112, 75, 124, 68, 84, 82, 60, 58, 122, 59, 123, 121, 65, 83, 81, 120, 64, 57, 80, 56, 92, 90, 91, 88, 89,
     ),
     (
-        12, 28, 52, 116, 11, 27, 51, 115, 48, 8, 24, 112, 49, 113, 9, 25, 50, 114, 44, 84, 60, 108, 124, 10, 26,
-        4, 83, 59, 3, 123, 80, 43, 40, 58, 107, 122, 91, 56, 104, 0, 81, 120, 1, 90, 42, 105, 41, 106, 2, 121,
-        57, 82, 36, 35, 76, 75, 92, 100, 99, 34, 98, 32, 72, 74, 33, 96, 73, 88, 89, 97, 68, 67, 66, 65, 64,
+        12, 28, 52, 116, 10, 26, 50, 114, 113, 9, 25, 49, 48, 112, 8, 24, 51, 115, 44, 108, 60, 124, 84, 11, 27,
+        4, 82, 58, 2, 122, 42, 41, 105, 59, 106, 123, 90, 121, 57, 1, 80, 81, 0, 91, 43, 40, 104, 107, 3, 56,
+        120, 83, 100, 76, 74, 92, 36, 34, 98, 35, 99, 97, 73, 75, 89, 96, 72, 33, 88, 32, 68, 66, 67, 64, 65,
     ),
     (
-        20, 60, 124, 19, 59, 123, 56, 16, 120, 57, 121, 17, 58, 122, 52, 92, 116, 18, 12, 91, 11, 51, 115, 48, 112,
-        8, 88, 89, 113, 9, 49, 90, 44, 84, 108, 50, 114, 10, 4, 40, 83, 80, 3, 43, 107, 41, 104, 0, 81, 36,
-        105, 76, 100, 73, 72, 1, 42, 106, 2, 32, 82, 96, 68, 35, 75, 99, 33, 34, 97, 98, 74, 67, 66, 64, 65,
+        20, 60, 124, 18, 58, 122, 121, 17, 57, 56, 120, 16, 59, 123, 52, 116, 92, 19, 12, 90, 10, 50, 114, 113, 49,
+        9, 89, 88, 48, 8, 112, 91, 108, 84, 44, 51, 115, 11, 4, 105, 82, 81, 2, 42, 106, 104, 41, 1, 80, 100,
+        40, 76, 36, 72, 73, 0, 43, 107, 3, 97, 83, 33, 68, 74, 34, 98, 96, 35, 32, 99, 75, 66, 67, 65, 64,
     ),
 )
 EARLY = 14
@@ -114,7 +114,7 @@
     beside = dx == (X - 1 if even else 1)
     no = z < 0
     if piece == RANKS:
-        return (here & up, here & down, here | beside, here), (no,) * 4
+        return (here & up, here & down, here, here | (dx == 1)), (no,) * 4
     if piece < 2:
         if even:
             return (here & up, here & down, here, no), (no, no, beside, here)
@@ -191,7 +191,7 @@
         load(5, w_hbm.at[:, pl.ds(HALF, HALF)], wbuf.at[:, pl.ds(HALF, HALF)]),
         load(6, h_hbm.at[:, core], hbuf.at[1]),
     ]
-    for copy in loads:
+    for copy in loads[:3]:
         copy.start()
 
     barrier = pltpu.get_barrier_semaphore()
@@ -215,6 +215,9 @@
         @pl.loop(0, CHIPS)
         def _(q):
             greet((above, q * CORES + core))
+
+    for copy in loads[3:]:
+        copy.start()
 
     loads[1].wait()
     loads[2].wait()
@@ -328,7 +331,7 @@
 
     pass_on(chip, RANKS)
     loads[0].wait()
-    for piece in (3, 0, 1, 2):
+    for piece in (2, 1, 0, 3):
         pass_on(chip, piece)
     picked_down = remote(picked_v, pk, pk_send, pk_recv, (below, me))
 
@@ -420,12 +423,6 @@
     other = pl.ds(pl.multiple_of((1 - core) * RANK_ROWS, RANK_ROWS), RANK_ROWS)
     other_rows = remote(rn.at[other], rn.at[other], r_send.at[4], r_recv.at[4], sibling)
 
-    @pl.when(s < sections - 1)
-    def _():
-        router_down.wait_recv()
-        for copy in spreads:
-            copy.start()
-
     for half in range(2):
         crossing(half).wait_recv()
     acc[...] = jnp.zeros_like(acc)
@@ -489,7 +486,13 @@
         def _():
             finish(q)
 
-        @pl.when((i == COUNT // 2) & (s < sections - 1))
+        @pl.when((i == COUNT // 4) & (s < sections - 1))
+        def _():
+            router_down.wait_recv()
+            for copy in spreads:
+                copy.start()
+
+        @pl.when((i == 3 * COUNT // 4) & (s < sections - 1))
         def _():
             came(0, left).wait_recv()
             came(1, right).wait_recv()
@@ -501,13 +504,13 @@
         other_rows.wait_recv()
         rn_out[...] = rn[...]
         picked_down.wait_recv()
-
+        picked = pk[...]
+        weight = picked / jnp.sum(picked, axis=0, keepdims=True)
+        slope = weight * (1.0 - picked)
         remote(sent_scores, st, score_send, score_recv, (below, me)).wait_recv()
-        picked = pk[...]
         score_grad = jnp.concatenate([st[q] for q in range(CHIPS)], axis=0)
-        picked_sum = jnp.sum(picked, axis=0, keepdims=True)
-        mean_grad = jnp.sum(picked / picked_sum * score_grad, axis=0, keepdims=True)
-        table = (score_grad - mean_grad) / picked_sum * picked * (1.0 - picked)
+        mean_grad = jnp.sum(weight * score_grad, axis=0, keepdims=True)
+        table = (score_grad - mean_grad) * slope
         square = jnp.concatenate([table, jnp.zeros((TOK - EXPERTS, TOK), F32)], axis=0)
         table_out[...] = square.T[:, :EXPERTS].astype(BF16)
 

time: 105 us -> 105 us (level)
  no operation moved by 1% of the time
where the time goes in v6:
time: 105 us; the launch traced here: 104 us
  Pallas kernels  103 us (98%)
  matrix products  1.3 us (1%)
    pallas_call x1, Pallas kernels, exchange(): pl.pallas_call(kernel, out_shape=(jax.ShapeDtypeStruct((TOK, EXPERTS), BF...  103 us

profile of v6, /device:TPU:8, one launch (start us, length us, event | category | flops | bytes accessed | tf_op | source)
XLA Modules:
  0.0 104.4 jit_solution(7371535538148570714)
XLA Ops:
  0.0 103.1 %shard_map.64 = (bf16[128,32]{1,0:T(8,128)(2,1)S(1)}, bf16[32,3584]{1,0:T(8,128)(2,1)S(1)}) custom-call(bf16[128,3584]{1,0:T(8,128)(2,1)} %bitcast.16, s32[8,128]{1,0:T(8,128)} %bitcast.19, f32[32,128]{1,0:T(8,128)} %bitcast.18, bf16[16,2,48,1024]{3,2,1,0:T(8,128)(2,1)} %bitcast.15, bf16[1024,3584]{1,0:T(8,128)(2,1)} %bitcast.14, bf16[32,3584]{1,0:T(8,128)(2,1)} %bitcast.17), custom_call_target="tpu_custom_call" | custom-call | tf_op jit(solution)/shard_map/pallas_call | solution.py:553
  103.1 1.3 %fusion = bf16[1,128,3584]{2,1,0:T(8,128)(2,1)} fusion(bf16[128,32]{1,0:T(8,128)(2,1)S(1)} %get-tuple-element.7, bf16[32,3584]{1,0:T(8,128)(2,1)S(1)} %get-tuple-element.8), kind=kOutput, calls=%fused_computation.1 | convolution fusion | flops 29818880 | bytes 1155072 | tf_op jit(solution)/shard_map/dot_general | solution.py:602

commit v7 on v6

--- a/solution.py
+++ b/solution.py
@@ -152,9 +152,9 @@
     g_hbm, ids_hbm, logits_hbm, h_hbm, w_hbm, r_hbm,
     table_out, rn_out,
     held, ranks_of, wide_rows, slim_rows, prod, cross, hbuf, wbuf, acc, slot_acc, sent_scores,
-    ids_v, logits_v, picked_v, st, rn, pk,
+    ids_v, logits_v, picked_v, st, rn, pk, next_ids,
     load_sem, send_sem, recv_sem, cross_send, cross_recv,
-    score_send, score_recv, r_send, r_recv, pk_send, pk_recv,
+    score_send, score_recv, r_send, r_recv, pk_send, pk_recv, ids_send, ids_recv,
 ):
     sections = lax.axis_size("pp")
     s = lax.axis_index("pp")
@@ -234,7 +234,9 @@
     ranks = jnp.where(named > 0, before, -1.0).astype(BF16)
     ranks_of[chip] = jnp.concatenate([ranks[:RANK_ROWS], ranks[RANK_ROWS:]], axis=1)
     affinity = 1.0 / (1.0 + jnp.exp(-logits_v[...]))
-    picked_v[...] = jnp.where(named > 0, affinity, 0.0)
+    for k in range(ids.shape[0]):
+        mine = jnp.where(ids[k : k + 1] == experts, affinity, 0.0)
+        picked_v[k : k + 1, :] = jnp.sum(mine, axis=0, keepdims=True)
 
     calls = 4 + (z < Z - 1).astype(jnp.int32) + (z > 0).astype(jnp.int32)
     calls = calls + CHIPS * (s > 0).astype(jnp.int32)
@@ -334,10 +336,12 @@
     for piece in (2, 1, 0, 3):
         pass_on(chip, piece)
     picked_down = remote(picked_v, pk, pk_send, pk_recv, (below, me))
+    ids_down = remote(ids_v, next_ids, ids_send, ids_recv, (below, me))
 
     @pl.when(s > 0)
     def _():
         picked_down.start()
+        ids_down.start()
 
     steps = [by_row(z, words) for words in zip(*map(packed, STEPS))]
     early = [by_row(z, words) for words in zip(*(packed(row[:EARLY]) for row in ORDER))]
@@ -504,7 +508,10 @@
         other_rows.wait_recv()
         rn_out[...] = rn[...]
         picked_down.wait_recv()
-        picked = pk[...]
+        ids_down.wait_recv()
+        picked = jnp.zeros((EXPERTS, TOK), F32)
+        for k in range(ids.shape[0]):
+            picked = picked + jnp.where(next_ids[k : k + 1, :] == experts, pk[k : k + 1, :], 0.0)
         weight = picked / jnp.sum(picked, axis=0, keepdims=True)
         slope = weight * (1.0 - picked)
         remote(sent_scores, st, score_send, score_recv, (below, me)).wait_recv()
@@ -532,6 +539,7 @@
     def _():
         router_down.wait_send()
         picked_down.wait_send()
+        ids_down.wait_send()
         remote(sent_scores, st, score_send, score_recv, (below, me)).wait_send()
 
     for row in range(Z):
@@ -572,10 +580,11 @@
             pltpu.VMEM((CHIPS, CORES, TOK), F32),
             pltpu.VMEM(ids.shape, jnp.int32),
             pltpu.VMEM(logits.shape, F32),
-            pltpu.VMEM((EXPERTS, TOK), F32),
+            pltpu.VMEM(ids.shape, F32),
             pltpu.VMEM((CHIPS, CORES, TOK), F32),
             pltpu.VMEM((EXPERTS, D), BF16),
-            pltpu.VMEM((EXPERTS, TOK), F32),
+            pltpu.VMEM(ids.shape, F32),
+            pltpu.VMEM(ids.shape, jnp.int32),
             dma((7,)),
             dma((len(GROUPS),)),
             dma((CHIPS, 5)),
@@ -585,6 +594,8 @@
             dma,
             dma((5,)),
             dma((5,)),
+            dma,
+            dma,
             dma,
             dma,
         ],

time: 105 us -> 105 us (level)
  no operation moved by 1% of the time
where the time goes in v7:
time: 105 us; the launch traced here: 104 us
  Pallas kernels  103 us (98%)
  matrix products  1.29 us (1%)
    pallas_call x1, Pallas kernels, exchange(): pl.pallas_call(kernel, out_shape=(jax.ShapeDtypeStruct((TOK, EXPERTS), BF...  103 us

profile of v7, /device:TPU:8, one launch (start us, length us, event | category | flops | bytes accessed | tf_op | source)
XLA Modules:
  0.0 104.5 jit_solution(5654280047924504548)
XLA Ops:
  0.0 103.2 %shard_map.64 = (bf16[128,32]{1,0:T(8,128)(2,1)S(1)}, bf16[32,3584]{1,0:T(8,128)(2,1)S(1)}) custom-call(bf16[128,3584]{1,0:T(8,128)(2,1)} %bitcast.16, s32[8,128]{1,0:T(8,128)} %bitcast.19, f32[32,128]{1,0:T(8,128)} %bitcast.18, bf16[16,2,48,1024]{3,2,1,0:T(8,128)(2,1)} %bitcast.15, bf16[1024,3584]{1,0:T(8,128)(2,1)} %bitcast.14, bf16[32,3584]{1,0:T(8,128)(2,1)} %bitcast.17), custom_call_target="tpu_custom_call" | custom-call | tf_op jit(solution)/shard_map/pallas_call | solution.py:561
  103.2 1.3 %fusion = bf16[1,128,3584]{2,1,0:T(8,128)(2,1)} fusion(bf16[128,32]{1,0:T(8,128)(2,1)S(1)} %get-tuple-element.7, bf16[32,3584]{1,0:T(8,128)(2,1)S(1)} %get-tuple-element.8), kind=kOutput, calls=%fused_computation.1 | convolution fusion | flops 29818880 | bytes 1155072 | tf_op jit(solution)/shard_map/dot_general | solution.py:613
